TPU v7x, 32 devices: a whole 2x2x4 slice. The times are simulated.
32 devices in a mesh: dp: 8 (over z, y), tensor: 4 (over x, core).
Axes of the slice: x: 2, y: 2, z: 4, core: 2. Of those that a mesh axis runs over, the one named last changes fastest.
Arguments:
- hidden: bfloat16 [8192, 768], P(('dp', 'tensor'))
- long_lengths: int32 [8], P('dp'), may hold values from 128 to 512, as said below
- short_lengths: int32 [32], P('dp'), may hold values from 32 to 128, as said below
- w_qkv: bfloat16 [2, 3, 768, 768], P(None, None, None, 'tensor'), may hold values from -0.3125 to 0.3125
- bias_qv: float32 [2, 2, 768], P(None, None, 'tensor'), may hold values from -3 to 3
- w_out: bfloat16 [2, 768, 768], P(None, 'tensor'), may hold values from -1.25 to 1.25
- bias_out: float32 [2, 768], replicated, may hold values from -3 to 3
- ln_gain: float32 [2, 2, 768], replicated, may hold values from 0.25 to 1.75
- ln_bias: float32 [2, 2, 768], replicated, may hold values from -2 to 2
- w_up: bfloat16 [2, 768, 3072], P(None, None, 'tensor'), may hold values from -0.21875 to 0.21875
- bias_up: float32 [2, 3072], P(None, 'tensor'), may hold values from -3 to 3
- w_down: bfloat16 [2, 3072, 768], P(None, 'tensor'), may hold values from -0.21875 to 0.21875
- bias_down: float32 [2, 768], replicated, may hold values from -3 to 3
- cotangent: bfloat16 [8192, 768], P(('dp', 'tensor')), may hold values from -6 to 6
Outputs:
- hidden_out: bfloat16 [8192, 768], P(('dp', 'tensor'))
- grad_hidden: float32 [8192, 768], P(('dp', 'tensor'))
- grad_qkv: float32 [2, 3, 768, 768], P(None, None, 'dp', 'tensor')
- grad_bias_qv: float32 [2, 2, 768], P(None, None, 'tensor')
- grad_out: float32 [2, 768, 768], P(None, 'tensor', 'dp')
- grad_bias_out: float32 [2, 768], replicated
- grad_ln_gain: float32 [2, 2, 768], replicated
- grad_ln_bias: float32 [2, 2, 768], replicated
- grad_up: float32 [2, 768, 3072], P(None, 'dp', 'tensor')
- grad_bias_up: float32 [2, 3072], P(None, 'tensor')
- grad_down: float32 [2, 3072, 768], P(None, 'tensor', 'dp')
- grad_bias_down: float32 [2, 768], replicated
- rms_values: float32 [2, 3], replicated
Inputs may be any that keep to these rules, and one draw needn't show every extreme that they name: `long_lengths`: live leading slots of each long row of 512; row 0 is full. `short_lengths`: live leading slots of each short row of 128; row 0 is full.
All inputs are finite; a program needn't handle non-finite values. Where the computation divides by a largest or mean magnitude, that divisor is 1e-20 or more.
Results may differ from a plain program's by a relative error of at most 0.035.
Values may be sent and summed in bfloat16 or wider, within the bound.
No kernel may reach another device: no remote copies, remote signals or barrier semaphores. Data moves between devices by JAX's collectives and lax.ppermute only.
A program may use at most 192 MiB of HBM per device.

v0:
```python
from functools import partial

import jax
import jax.numpy as jnp
from jax import lax
from jax.sharding import PartitionSpec as P

HEAD_DIM = 64
LAYERS = 2
LONG_LEN = 512
SHORT_LEN = 128
LONG_DEV = 1
SHORT_DEV = 4


eps_norm = 1e-06
eps_clip = 1e-06


def layer_norm(values, gain_row, shift_row):
    centre = jnp.mean(values, axis=-1, keepdims=True)
    spread = jnp.mean((values - centre) ** 2, axis=-1, keepdims=True)
    return (values - centre) * lax.rsqrt(spread + eps_norm) * gain_row + shift_row


def global_top(values):
    return lax.pmax(jnp.max(jnp.abs(values)), ("dp", "tensor"))


def gather_inputs(values):
    return lax.all_gather(values, "tensor", axis=0, tiled=True)


def gather_grads(values):
    return lax.all_gather(values, "tensor", axis=0, tiled=True)


def gather_again(values):
    return lax.all_gather(values, "tensor", axis=0, tiled=True)


def forward_rows(left_side, right_side, row_count):

    def row_term(begin_row, span_rows):
        return jnp.dot(left_side, right_side, preferred_element_type=jnp.float32)

    return lax.psum_scatter(
        row_term(jnp.int32(0), row_count * lax.axis_size("tensor")),
        "tensor",
        scatter_dimension=0,
        tiled=True,
    )


def backward_rows(row_term, row_count):
    return lax.psum_scatter(
        row_term(jnp.int32(0), lax.axis_size("tensor") * row_count).astype(jnp.bfloat16),
        "tensor",
        scatter_dimension=0,
        tiled=True,
    ).astype(jnp.float32)


def clip_forward(values, largest):
    clip_bound = largest * 0.25 + eps_clip
    tangent = jnp.tanh(values / clip_bound)
    return (clip_bound * tangent, tangent)


def clip_backward(grad_in, tangent):
    return grad_in * (1.0 - tangent * tangent)


def split_rows(rows_in, head_count):
    cut_point = LONG_DEV * LONG_LEN
    long_part = rows_in[:cut_point].reshape(LONG_DEV, LONG_LEN, head_count, HEAD_DIM)
    short_part = rows_in[cut_point:].reshape(SHORT_DEV, SHORT_LEN, head_count, HEAD_DIM)
    return (long_part, short_part)


def join_rows(long_part, short_part):
    row_width = long_part.shape[2] * long_part.shape[3]
    return jnp.concatenate([long_part.reshape(-1, row_width), short_part.reshape(-1, row_width)], 0)


def group_scores(queries, key_rows, lengths):
    scores = jnp.einsum(
        "bqhd,bkhd->bhqk", queries, key_rows, preferred_element_type=jnp.float32
    ) * HEAD_DIM ** (-0.5)
    live = (
        jnp.arange(key_rows.shape[1], dtype=jnp.int32)[None, None, None, :]
        < lengths[:, None, None, None]
    )
    return jnp.where(live, scores, -1000000000.0)


def group_forward(queries, key_rows, value_rows, lengths):
    scores = group_scores(queries, key_rows, lengths)
    top_score = jnp.max(scores, axis=-1, keepdims=True)
    weights = jnp.exp(scores - top_score)
    weight_sum = jnp.sum(weights, axis=-1, keepdims=True)
    probs = weights / weight_sum
    log_total = top_score + jnp.log(weight_sum)
    context = jnp.einsum(
        "bhqk,bkhd->bqhd",
        probs.astype(jnp.bfloat16),
        value_rows,
        preferred_element_type=jnp.float32,
    )
    return (context, log_total)


def group_backward(queries, key_rows, value_rows, lengths, log_total, grad_context):
    scores = group_scores(queries, key_rows, lengths)
    probs = jnp.exp(scores - log_total)
    grad_probs = jnp.einsum(
        "bqhd,bkhd->bhqk", grad_context, value_rows, preferred_element_type=jnp.float32
    )
    grad_values = jnp.einsum(
        "bhqk,bqhd->bkhd",
        probs.astype(jnp.bfloat16),
        grad_context,
        preferred_element_type=jnp.float32,
    )
    grad_scores = (
        probs * (grad_probs - jnp.sum(probs * grad_probs, axis=-1, keepdims=True))
    ).astype(jnp.bfloat16)
    scale = HEAD_DIM ** (-0.5)
    grad_queries = (
        jnp.einsum("bhqk,bkhd->bqhd", grad_scores, key_rows, preferred_element_type=jnp.float32)
        * scale
    )
    grad_keys = (
        jnp.einsum("bhqk,bqhd->bkhd", grad_scores, queries, preferred_element_type=jnp.float32)
        * scale
    )
    return (grad_queries, grad_keys, grad_values)


def body(
    hidden,
    long_lengths,
    short_lengths,
    w_qkv,
    bias_qv,
    w_out,
    bias_out,
    ln_gain,
    ln_bias,
    w_up,
    bias_up,
    w_down,
    bias_down,
    cotangent,
):
    row_count = hidden.shape[0]
    model_width = hidden.shape[1]
    head_count = w_qkv.shape[-1] // HEAD_DIM
    device_count = lax.axis_size("dp") * lax.axis_size("tensor")
    count_model = float(row_count * device_count * model_width)
    states = hidden.astype(jnp.float32)
    saved_layers = []
    square_terms = []
    for layer_index in range(LAYERS):
        input_square = jnp.sum(states * states)
        clipped_in, tangent_in = clip_forward(states, global_top(states))
        inputs_low = clipped_in.astype(jnp.bfloat16)
        gathered_in = gather_inputs(inputs_low)
        projected = jnp.einsum(
            "td,kde->kte", gathered_in, w_qkv[layer_index], preferred_element_type=jnp.float32
        )
        queries = (projected[0] + bias_qv[layer_index, 0]).astype(jnp.bfloat16)
        key_rows = projected[1].astype(jnp.bfloat16)
        value_rows = (projected[2] + bias_qv[layer_index, 1]).astype(jnp.bfloat16)
        long_query, short_query = split_rows(queries, head_count)
        long_key, short_key = split_rows(key_rows, head_count)
        long_value, short_value = split_rows(value_rows, head_count)
        long_context, long_total = group_forward(long_query, long_key, long_value, long_lengths)
        short_context, short_total = group_forward(
            short_query, short_key, short_value, short_lengths
        )
        context = join_rows(long_context, short_context)
        clipped_ctx, tangent_ctx = clip_forward(context, global_top(context))
        context_low = clipped_ctx.astype(jnp.bfloat16)
        branch = forward_rows(context_low, w_out[layer_index], row_count) + bias_out[layer_index]
        mixed = states + branch
        middle = layer_norm(mixed, ln_gain[layer_index, 0], ln_bias[layer_index, 0])
        clipped_mid, tangent_mid = clip_forward(middle, global_top(middle))
        middle_low = clipped_mid.astype(jnp.bfloat16)
        gathered_mid = gather_inputs(middle_low)
        hidden_units = (
            jnp.dot(gathered_mid, w_up[layer_index], preferred_element_type=jnp.float32)
            + bias_up[layer_index]
        )
        active = jax.nn.gelu(hidden_units, approximate=False)
        clipped_act, tangent_act = clip_forward(active, global_top(active))
        active_low = clipped_act.astype(jnp.bfloat16)
        branch_ffn = (
            forward_rows(active_low, w_down[layer_index], row_count) + bias_down[layer_index]
        )
        mixed_ffn = middle + branch_ffn
        square_terms.append(
            jnp.stack([input_square, jnp.sum(branch * branch), jnp.sum(branch_ffn * branch_ffn)])
        )
        saved_layers.append(
            (
                tangent_in,
                inputs_low,
                gathered_in,
                queries,
                key_rows,
                value_rows,
                long_total,
                short_total,
                tangent_ctx,
                context_low,
                mixed,
                tangent_mid,
                middle_low,
                gathered_mid,
                hidden_units,
                tangent_act,
                active_low,
                mixed_ffn,
            )
        )
        states = layer_norm(mixed_ffn, ln_gain[layer_index, 1], ln_bias[layer_index, 1])
    output = states.astype(jnp.bfloat16)
    grad_states = cotangent.astype(jnp.float32)
    qkv_list = [None] * LAYERS
    out_list = [None] * LAYERS
    up_list = [None] * LAYERS
    down_list = [None] * LAYERS
    head_bias_list = [None] * LAYERS
    unit_bias_list = [None] * LAYERS
    out_bias_list = [None] * LAYERS
    down_bias_list = [None] * LAYERS
    gain_list = [None] * LAYERS
    shift_list = [None] * LAYERS
    for layer_index in reversed(range(LAYERS)):
        (
            tangent_in,
            inputs_low,
            gathered_in,
            queries,
            key_rows,
            value_rows,
            long_total,
            short_total,
            tangent_ctx,
            context_low,
            mixed,
            tangent_mid,
            middle_low,
            gathered_mid,
            hidden_units,
            tangent_act,
            active_low,
            mixed_ffn,
        ) = saved_layers[layer_index]
        norm_out, norm_pull = jax.vjp(
            layer_norm, mixed_ffn, ln_gain[layer_index, 1], ln_bias[layer_index, 1]
        )
        grad_mixed_ffn, gain_two, shift_two = norm_pull(grad_states)
        ffn_low = grad_mixed_ffn.astype(jnp.bfloat16)
        down_bias_list[layer_index] = jnp.sum(ffn_low, axis=0, dtype=jnp.float32)
        ffn_rows = gather_grads(ffn_low)
        grad_active_low = jnp.einsum(
            "td,fd->tf", ffn_rows, w_down[layer_index], preferred_element_type=jnp.float32
        )
        down_grad = jnp.einsum(
            "tf,td->fd", active_low, ffn_rows, preferred_element_type=jnp.float32
        )
        grad_active = clip_backward(grad_active_low, tangent_act)
        gelu_out, gelu_pull = jax.vjp(partial(jax.nn.gelu, approximate=False), hidden_units)
        (grad_units,) = gelu_pull(grad_active)
        units_low = grad_units.astype(jnp.bfloat16)
        unit_bias_list[layer_index] = jnp.sum(units_low, axis=0, dtype=jnp.float32)
        middle_rows = gather_again(middle_low)
        up_grad = jnp.einsum(
            "td,tf->df", middle_rows, units_low, preferred_element_type=jnp.float32
        )

        def up_term(begin_row, span_rows):
            return jnp.einsum(
                "tf,df->td", units_low, w_up[layer_index], preferred_element_type=jnp.float32
            )

        grad_middle_low = backward_rows(up_term, row_count)
        grad_middle = clip_backward(grad_middle_low, tangent_mid) + grad_mixed_ffn
        norm_out, norm_pull = jax.vjp(
            layer_norm, mixed, ln_gain[layer_index, 0], ln_bias[layer_index, 0]
        )
        grad_mixed, gain_one, shift_one = norm_pull(grad_middle)
        gain_list[layer_index] = jnp.stack([gain_one, gain_two])
        shift_list[layer_index] = jnp.stack([shift_one, shift_two])
        branch_low = grad_mixed.astype(jnp.bfloat16)
        out_bias_list[layer_index] = jnp.sum(branch_low, axis=0, dtype=jnp.float32)
        branch_rows = gather_grads(branch_low)
        grad_context_low = jnp.einsum(
            "td,ed->te", branch_rows, w_out[layer_index], preferred_element_type=jnp.float32
        )
        out_grad = jnp.einsum(
            "te,td->ed", context_low, branch_rows, preferred_element_type=jnp.float32
        )
        grad_context = clip_backward(grad_context_low, tangent_ctx).astype(jnp.bfloat16)
        long_query, short_query = split_rows(queries, head_count)
        long_key, short_key = split_rows(key_rows, head_count)
        long_value, short_value = split_rows(value_rows, head_count)
        long_grad, short_grad = split_rows(grad_context, head_count)
        long_dq, long_dk, long_dv = group_backward(
            long_query, long_key, long_value, long_lengths, long_total, long_grad
        )
        short_dq, short_dk, short_dv = group_backward(
            short_query, short_key, short_value, short_lengths, short_total, short_grad
        )
        grad_queries = join_rows(long_dq, short_dq).astype(jnp.bfloat16)
        grad_keys = join_rows(long_dk, short_dk).astype(jnp.bfloat16)
        grad_values = join_rows(long_dv, short_dv).astype(jnp.bfloat16)
        head_bias_list[layer_index] = jnp.stack(
            [
                jnp.sum(grad_queries, axis=0, dtype=jnp.float32),
                jnp.sum(grad_values, axis=0, dtype=jnp.float32),
            ]
        )
        stacked = jnp.stack([grad_queries, grad_keys, grad_values])
        input_rows = gather_again(inputs_low)
        qkv_grad = jnp.einsum(
            "td,kte->kde", input_rows, stacked, preferred_element_type=jnp.float32
        )

        def qkv_term(begin_row, span_rows):
            return jnp.einsum(
                "kte,kde->td", stacked, w_qkv[layer_index], preferred_element_type=jnp.float32
            )

        grad_inputs_low = backward_rows(qkv_term, row_count)
        grad_states = clip_backward(grad_inputs_low, tangent_in) + grad_mixed
        qkv_list[layer_index] = qkv_grad
        out_list[layer_index] = out_grad
        up_list[layer_index] = up_grad
        down_list[layer_index] = down_grad
    qkv_all, out_all, up_all, down_all = (
        lax.psum_scatter(jnp.stack(qkv_list), "dp", scatter_dimension=2, tiled=True),
        lax.psum_scatter(jnp.stack(out_list), "dp", scatter_dimension=2, tiled=True),
        lax.psum_scatter(jnp.stack(up_list), "dp", scatter_dimension=1, tiled=True),
        lax.psum_scatter(jnp.stack(down_list), "dp", scatter_dimension=2, tiled=True),
    )
    head_bias_all, unit_bias_all = lax.psum(
        (jnp.stack(head_bias_list), jnp.stack(unit_bias_list)), "dp"
    )
    out_bias_all, down_bias_all, gain_all, shift_all, square_all = lax.psum(
        (
            jnp.stack(out_bias_list),
            jnp.stack(down_bias_list),
            jnp.stack(gain_list),
            jnp.stack(shift_list),
            jnp.stack(square_terms),
        ),
        ("dp", "tensor"),
    )
    rms_values = jnp.sqrt(square_all / count_model)
    return (
        output,
        grad_states,
        qkv_all,
        head_bias_all,
        out_all,
        out_bias_all,
        gain_all,
        shift_all,
        up_all,
        unit_bias_all,
        down_all,
        down_bias_all,
        rms_values,
    )


def solution(mesh):
    in_specs = (
        P(("dp", "tensor"), None),
        P("dp"),
        P("dp"),
        P(None, None, None, "tensor"),
        P(None, None, "tensor"),
        P(None, "tensor", None),
        P(),
        P(),
        P(),
        P(None, None, "tensor"),
        P(None, "tensor"),
        P(None, "tensor", None),
        P(),
        P(("dp", "tensor"), None),
    )
    out_specs = (
        P(("dp", "tensor"), None),
        P(("dp", "tensor"), None),
        P(None, None, "dp", "tensor"),
        P(None, None, "tensor"),
        P(None, "tensor", "dp"),
        P(),
        P(),
        P(),
        P(None, "dp", "tensor"),
        P(None, "tensor"),
        P(None, "tensor", "dp"),
        P(),
        P(),
    )
    return jax.shard_map(body, mesh=mesh, in_specs=in_specs, out_specs=out_specs, check_vma=False)
```

profile of v0, /device:TPU:0, one launch (start us, length us, event | category | flops | bytes accessed | tf_op | source)
XLA Modules:
  0.0 1340.1 jit_solution(11207574801477334401)
XLA Ops:
  9.0 42.2 %pmax.56 = f32[]{:T(128)} all-reduce(f32[]{:T(128)} %get-tuple-element.70), channel_id=1, replica_groups=mesh['dp'=8,'tensor'=4] {'dp','tensor'}, use_global_device_ids=true, to_apply=%region_1.0 | all-reduce | flops 1 | bytes 8 | tf_op jit(solution)/shard_map/pmax | solution.py:27
  82.1 39.5 %pmax.57 = f32[]{:T(128)} all-reduce(f32[]{:T(128)} %abs_reduce_fusion.6), channel_id=1, replica_groups=mesh['dp'=8,'tensor'=4] {'dp','tensor'}, use_global_device_ids=true, to_apply=%region_7.8 | all-reduce | flops 1 | bytes 8 | tf_op jit(solution)/shard_map/pmax | solution.py:27
  126.6 37.1 %reduce-scatter.16.cloned.1.call-done = f32[256,768]{1,0:T(8,128)} async-done(((f32[1024,768]{1,0:T(8,128)}), f32[256,768]{1,0:T(8,128)}) %reduce-scatter.16.cloned.1.call-update) | async-done | bytes 786448 | tf_op jit(solution)/shard_map/reduce_scatter | solution.py:47
  166.7 39.5 %pmax.58 = f32[]{:T(128)} all-reduce(f32[]{:T(128)} %abs_reduce_fusion.5), channel_id=1, replica_groups=mesh['dp'=8,'tensor'=4] {'dp','tensor'}, use_global_device_ids=true, to_apply=%region_12.13 | all-reduce | flops 1 | bytes 8 | tf_op jit(solution)/shard_map/pmax | solution.py:27
  241.0 39.5 %pmax.59 = f32[]{:T(128)} all-reduce(f32[]{:T(128)} %get-tuple-element.115), channel_id=1, replica_groups=mesh['dp'=8,'tensor'=4] {'dp','tensor'}, use_global_device_ids=true, to_apply=%region_14.15 | all-reduce | flops 1 | bytes 8 | tf_op jit(solution)/shard_map/pmax | solution.py:27
  290.4 37.8 %reduce-scatter.18.cloned.1.call-done = f32[256,768]{1,0:T(8,128)} async-done(((f32[1024,768]{1,0:T(8,128)}), f32[256,768]{1,0:T(8,128)}) %reduce-scatter.18.cloned.1.call-update) | async-done | bytes 786448 | tf_op jit(solution)/shard_map/reduce_scatter | solution.py:47
  331.6 39.5 %pmax.60 = f32[]{:T(128)} all-reduce(f32[]{:T(128)} %get-tuple-element.61), channel_id=1, replica_groups=mesh['dp'=8,'tensor'=4] {'dp','tensor'}, use_global_device_ids=true, to_apply=%region_19.20 | all-reduce | flops 1 | bytes 8 | tf_op jit(solution)/shard_map/pmax | solution.py:27
  373.1 20.6 %all-gather.13.cloned.1.call-done = bf16[1024,768]{1,0:T(8,128)(2,1)} async-done(((bf16[256,768]{1,0:T(8,128)(2,1)}), bf16[1024,768]{1,0:T(8,128)(2,1)}) %all-gather.13.cloned.1.call-update) | async-done | bytes 1572880 | tf_op jit(solution)/shard_map/all_gather | solution.py:31
  401.4 39.5 %pmax.61 = f32[]{:T(128)} all-reduce(f32[]{:T(128)} %abs_reduce_fusion.3), channel_id=1, replica_groups=mesh['dp'=8,'tensor'=4] {'dp','tensor'}, use_global_device_ids=true, to_apply=%region_25.26 | all-reduce | flops 1 | bytes 8 | tf_op jit(solution)/shard_map/pmax | solution.py:27
  445.1 38.9 %reduce-scatter.20.cloned.1.call-done = f32[256,768]{1,0:T(8,128)} async-done(((f32[1024,768]{1,0:T(8,128)}), f32[256,768]{1,0:T(8,128)}) %reduce-scatter.20.cloned.1.call-update) | async-done | bytes 786448 | tf_op jit(solution)/shard_map/reduce_scatter | solution.py:47
  488.2 39.5 %pmax.62 = f32[]{:T(128)} all-reduce(f32[]{:T(128)} %abs_reduce_fusion.2), channel_id=1, replica_groups=mesh['dp'=8,'tensor'=4] {'dp','tensor'}, use_global_device_ids=true, to_apply=%region_30.31 | all-reduce | flops 1 | bytes 8 | tf_op jit(solution)/shard_map/pmax | solution.py:27
  530.6 20.7 %all-gather.15.cloned.1.call-done = bf16[1024,768]{1,0:T(8,128)(2,1)} async-done(((bf16[256,768]{1,0:T(8,128)(2,1)}), bf16[1024,768]{1,0:T(8,128)(2,1)}) %all-gather.15.cloned.1.call-update) | async-done | bytes 1572880 | tf_op jit(solution)/shard_map/all_gather | solution.py:31
  563.7 39.9 %pmax.63 = f32[]{:T(128)} all-reduce(f32[]{:T(128)} %get-tuple-element.109), channel_id=1, replica_groups=mesh['dp'=8,'tensor'=4] {'dp','tensor'}, use_global_device_ids=true, to_apply=%region_32.33 | all-reduce | flops 1 | bytes 8 | tf_op jit(solution)/shard_map/pmax | solution.py:27
  612.3 39.0 %reduce-scatter.22.cloned.1.call-done = f32[256,768]{1,0:T(8,128)} async-done(((f32[1024,768]{1,0:T(8,128)}), f32[256,768]{1,0:T(8,128)}) %reduce-scatter.22.cloned.1.call-update) | async-done | bytes 786448 | tf_op jit(solution)/shard_map/reduce_scatter | solution.py:47
  687.6 28.3 %reduce-scatter.24.cloned.1.call-done = bf16[256,768]{1,0:T(8,128)(2,1)} async-done(((bf16[1024,768]{1,0:T(8,128)(2,1)}), bf16[256,768]{1,0:T(8,128)(2,1)}) %reduce-scatter.24.cloned.1.call-update) | async-done | bytes 393232 | tf_op jit(solution)/shard_map/reduce_scatter | solution.py:56
  762.5 28.3 %reduce-scatter.26.cloned.1.call-done = bf16[256,768]{1,0:T(8,128)(2,1)} async-done(((bf16[1024,768]{1,0:T(8,128)(2,1)}), bf16[256,768]{1,0:T(8,128)(2,1)}) %reduce-scatter.26.cloned.1.call-update) | async-done | bytes 393232 | tf_op jit(solution)/shard_map/reduce_scatter | solution.py:56
  827.3 28.1 %reduce-scatter.28.cloned.1.call-done = bf16[256,768]{1,0:T(8,128)(2,1)} async-done(((bf16[1024,768]{1,0:T(8,128)(2,1)}), bf16[256,768]{1,0:T(8,128)(2,1)}) %reduce-scatter.28.cloned.1.call-update) | async-done | bytes 393232 | tf_op jit(solution)/shard_map/reduce_scatter | solution.py:56
  938.4 41.6 %all-reduce.1 = (f32[2,768]{1,0:T(2,128)}, f32[2,2,768]{2,1,0:T(2,128)}, f32[2,2,768]{2,1,0:T(2,128)}, f32[2,768]{1,0:T(2,128)}, f32[2,3]{1,0:T(2,128)S(1)}) all-reduce(f32[2,768]{1,0:T(2,128)S(1)} %pad_maximum_fusion.8, f32[2,2,768]{2,1,0:T(2,128)S(1)} %pad_maximum_fusion.6, ...), channel_id=1, replica_groups=mesh['dp'=8,'tensor'=4] {'dp','tensor'}, use_global_device_ids=true, to_apply=%region_65.66 | all-reduce | flops 9222 | bytes 73776 | tf_op jit(solution)/shard_map/psum | solution.py:352
  980.6 73.5 %all-reduce.5.cloned.1.call-done = f32[2,768,768]{1,0,2:T(2,128)} async-done(((f32[2,768,768]{1,0,2:T(2,128)}), f32[2,768,768]{1,0,2:T(2,128)}) %all-reduce.5.cloned.1.call-update) | async-done | bytes 4718608
  1056.4 35.2 %all-reduce.2 = (f32[2,2,192]{2,1,0:T(2,128)}, f32[2,768]{1,0:T(2,128)}) all-reduce(f32[2,2,192]{2,1,0:T(2,128)S(1)} %pad_maximum_fusion.11, f32[2,768]{1,0:T(2,128)S(1)} %pad_maximum_fusion.9), channel_id=1, replica_groups=mesh['dp'=8,'tensor'=4] {'dp'}, use_global_device_ids=true, to_apply=%region_61.62 | all-reduce | flops 2304 | bytes 18432 | tf_op jit(solution)/shard_map/psum | solution.py:349
  1091.6 29.2 %reduce-scatter.36.cloned.1.call-done = f32[96,384]{1,0:T(8,128)} async-done(((f32[768,384]{1,0:T(8,128)}), f32[96,384]{1,0:T(8,128)}) %reduce-scatter.36.cloned.1.call-update) | async-done | bytes 147472
  1122.7 27.9 %reduce-scatter.30.cloned.1.call-done = bf16[256,768]{1,0:T(8,128)(2,1)} async-done(((bf16[1024,768]{1,0:T(8,128)(2,1)}), bf16[256,768]{1,0:T(8,128)(2,1)}) %reduce-scatter.30.cloned.1.call-update) | async-done | bytes 393232 | tf_op jit(solution)/shard_map/reduce_scatter | solution.py:56
  1152.7 80.8 %reduce-scatter.34.cloned.1.call-done = f32[96,1152]{1,0:T(8,128)} async-done(((f32[768,1152]{1,0:T(8,128)}), f32[96,1152]{1,0:T(8,128)}) %reduce-scatter.34.cloned.1.call-update) | async-done | bytes 442384
  1236.0 96.7 %reduce-scatter.32.cloned.1.call-done = f32[2,96,768]{2,1,0:T(8,128)} async-done(((f32[2,768,768]{2,1,0:T(8,128)}), f32[2,96,768]{2,1,0:T(8,128)}) %reduce-scatter.32.cloned.1.call-update) | async-done | bytes 589840 | tf_op jit(solution)/shard_map/reduce_scatter | solution.py:346
  (579 shorter events, 333.6 us)
Async XLA Ops:
  7.2 66.4 %all-gather.9.cloned.1.call-start = ((), (), s32[]{:S(2)}) async-start(), calls=%async_computation.11 | async-start | bytes 1966080 | tf_op jit(solution)/shard_map/all_gather | solution.py:31
  53.8 109.9 %reduce-scatter.16.cloned.1.call-start = ((), (), s32[]{:S(2)}) async-start(), calls=%async_computation.12 | async-start | bytes 3932160 | tf_op jit(solution)/shard_map/reduce_scatter | solution.py:47
  124.7 104.1 %all-gather.11.cloned.1.call-start = ((), (), s32[]{:S(2)}) async-start(), calls=%async_computation.13 | async-start | bytes 1966080 | tf_op jit(solution)/shard_map/all_gather | solution.py:31
  126.6 201.6 %copy-start.85 = (f32[768]{0:T(1024)}, f32[768]{0:T(1024)S(1)}, u32[]{:S(2)}) copy-start(f32[768]{0:T(1024)S(1)} %get-tuple-element.78) | copy-start | bytes 9220
  126.6 357.5 %copy-start.87 = (f32[768]{0:T(1024)}, f32[768]{0:T(1024)S(1)}, u32[]{:S(2)}) copy-start(f32[768]{0:T(1024)S(1)} %get-tuple-element.77) | copy-start | bytes 9220
  208.0 120.2 %reduce-scatter.18.cloned.1.call-start = ((), (), s32[]{:S(2)}) async-start(), calls=%async_computation.14 | async-start | bytes 3932160 | tf_op jit(solution)/shard_map/reduce_scatter | solution.py:47
  289.2 104.5 %all-gather.13.cloned.1.call-start = ((), (), s32[]{:S(2)}) async-start(), calls=%async_computation.15 | async-start | bytes 1966080 | tf_op jit(solution)/shard_map/all_gather | solution.py:31
  372.8 111.3 %reduce-scatter.20.cloned.1.call-start = ((), (), s32[]{:S(2)}) async-start(), calls=%async_computation.16 | async-start | bytes 3932160 | tf_op jit(solution)/shard_map/reduce_scatter | solution.py:47
  445.1 106.2 %all-gather.15.cloned.1.call-start = ((), (), s32[]{:S(2)}) async-start(), calls=%async_computation.17 | async-start | bytes 1966080 | tf_op jit(solution)/shard_map/all_gather | solution.py:31
  530.6 120.7 %reduce-scatter.22.cloned.1.call-start = ((), (), s32[]{:S(2)}) async-start(), calls=%async_computation.18 | async-start | bytes 3932160 | tf_op jit(solution)/shard_map/reduce_scatter | solution.py:47
  612.2 64.3 %all-gather.17.cloned.1.call-start = ((), (), s32[]{:S(2)}) async-start(), calls=%async_computation.19 | async-start | bytes 1966080 | tf_op jit(solution)/shard_map/all_gather | solution.py:35
  656.8 59.1 %reduce-scatter.24.cloned.1.call-start = ((), (), s32[]{:S(2)}) async-start(), calls=%async_computation.20 | async-start | bytes 1966080 | tf_op jit(solution)/shard_map/reduce_scatter | solution.py:56
  687.5 54.1 %all-gather.19.cloned.1.call-start = ((), (), s32[]{:S(2)}) async-start(), calls=%async_computation.21 | async-start | bytes 1966080 | tf_op jit(solution)/shard_map/all_gather | solution.py:35
  721.9 68.9 %reduce-scatter.26.cloned.1.call-start = ((), (), s32[]{:S(2)}) async-start(), calls=%async_computation.22 | async-start | bytes 1966080 | tf_op jit(solution)/shard_map/reduce_scatter | solution.py:56
  762.5 52.4 %all-gather.21.cloned.1.call-start = ((), (), s32[]{:S(2)}) async-start(), calls=%async_computation.23 | async-start | bytes 1966080 | tf_op jit(solution)/shard_map/all_gather | solution.py:35
  795.0 60.4 %reduce-scatter.28.cloned.1.call-start = ((), (), s32[]{:S(2)}) async-start(), calls=%async_computation.24 | async-start | bytes 1966080 | tf_op jit(solution)/shard_map/reduce_scatter | solution.py:56
  827.1 52.7 %all-gather.23.cloned.1.call-start = ((), (), s32[]{:S(2)}) async-start(), calls=%async_computation.25 | async-start | bytes 1966080 | tf_op jit(solution)/shard_map/all_gather | solution.py:35
  860.0 194.1 %all-reduce.5.cloned.1.call-start = ((), (), s32[]{:S(2)}) async-start(), calls=%async_computation.30 | async-start | bytes 9437184
  875.3 245.6 %reduce-scatter.36.cloned.1.call-start = ((), (), s32[]{:S(2)}) async-start(), calls=%async_computation.29 | async-start | bytes 1327104
  894.6 256.0 %reduce-scatter.30.cloned.1.call-start = ((), (), s32[]{:S(2)}) async-start(), calls=%async_computation.26 | async-start | bytes 1966080 | tf_op jit(solution)/shard_map/reduce_scatter | solution.py:56
  906.5 327.0 %reduce-scatter.34.cloned.1.call-start = ((), (), s32[]{:S(2)}) async-start(), calls=%async_computation.28 | async-start | bytes 3981312
  923.5 409.2 %reduce-scatter.32.cloned.1.call-start = ((), (), s32[]{:S(2)}) async-start(), calls=%async_computation.27 | async-start | bytes 5308416 | tf_op jit(solution)/shard_map/reduce_scatter | solution.py:346
  937.7 212.9 %copy-start.14 = (bf16[256,768]{1,0:T(8,128)(2,1)S(1)}, bf16[256,768]{1,0:T(8,128)(2,1)}, u32[]{:S(2)}) copy-start(bf16[256,768]{1,0:T(8,128)(2,1)} %param.14) | copy-start | bytes 1179652
  937.7 212.9 %copy-start.16 = (f32[256,768]{1,0:T(8,128)S(1)}, f32[256,768]{1,0:T(8,128)}, u32[]{:S(2)}) copy-start(f32[256,768]{1,0:T(8,128)} %get-tuple-element.100) | copy-start | bytes 2359300
  (159 other events, 2898.7 us)
Sparse Core Ops, SparseCore 0:
  53.9 19.6 all-gather.8
  124.8 38.8 reduce-scatter.15
  208.1 20.5 all-gather.10
  289.3 38.8 reduce-scatter.17
  372.9 20.6 all-gather.12
  445.2 38.8 reduce-scatter.19
  530.7 20.5 all-gather.14
  612.4 38.8 reduce-scatter.21
  656.9 19.6 all-gather.16
  687.7 28.1 reduce-scatter.23
  722.0 19.6 all-gather.18
  762.6 28.1 reduce-scatter.25
  795.2 19.6 all-gather.20
  827.2 28.1 reduce-scatter.27
  860.1 19.6 all-gather.22
  883.7 170.3 all-reduce.4
  1057.7 63.1 reduce-scatter.35
  1123.4 27.1 reduce-scatter.29
  1154.2 79.1 reduce-scatter.33
  1237.5 95.1 reduce-scatter.31
where the time goes:
time: 1350 us; the launch traced here: 1340 us
  waiting for transfers between devices  682 us (51%)
  blocking collectives  396 us (29%)
  matrix products  110 us (8%)
  other arithmetic  66.5 us (5%)
  local copies, waits for them, and re-layouts  60.3 us (4%)
  between operations  23.7 us (2%)
    pmax x8, blocking collectives, global_top(): return lax.pmax(jnp.max(jnp.abs(values)), ('dp', 'tensor'))  319 us
    unnamed x23, waiting for transfers between devices  184 us
    reduce_scatter x4, waiting for transfers between devices, forward_rows(): lax.psum_scatter(row_term(jnp.int32(0), row_count * lax.axis_size('tensor...  153 us
    reduce_scatter x4, waiting for transfers between devices, backward_rows(): lax.psum_scatter(row_term(jnp.int32(0), lax.axis_size('tensor') * row_cou...  113 us
    reduce_scatter x1, waiting for transfers between devices, body(): lax.psum_scatter(jnp.stack(up_list), 'dp', scatter_dimension=1, tiled=True)  96.7 us
    all_gather x4, waiting for transfers between devices, gather_inputs(): return lax.all_gather(values, 'tensor', axis=0, tiled=True)  77.2 us
    all_gather x4, waiting for transfers between devices, gather_grads(): return lax.all_gather(values, 'tensor', axis=0, tiled=True)  58.6 us
    psum x1, blocking collectives, body(): lax.psum((jnp.stack(out_bias_list), jnp.stack(down_bias_list), jnp.stack(...  41.6 us
  transfers between devices with their start and end apart: 20, of which 20 were waited for; matrix products, arithmetic and copies ran while one was open for 7% of the time, Pallas kernels for 0%

commit v1 on v0

v1 whole, which is shorter than its diff:
```python
from functools import partial

import jax
import jax.numpy as jnp
from jax import lax
from jax.experimental import pallas as pl
from jax.experimental.pallas import tpu as pltpu
from jax.sharding import PartitionSpec as P

HEAD_DIM = 64
LAYERS = 2
LONG_LEN = 512
SHORT_LEN = 128
LONG_DEV = 1
SHORT_DEV = 4

EPS = 1e-06
MASKED = -1e30
BOTH = ("dp", "tensor")
F32 = jnp.float32
BF16 = jnp.bfloat16
VMEM_LIMIT = 40 * 1024 * 1024


def nt(left, right):
    return lax.dot_general(left, right, (((1,), (1,)), ((), ())), preferred_element_type=F32)


def nn(left, right):
    return jnp.dot(left, right, preferred_element_type=F32)


def tn(left, right):
    return lax.dot_general(left, right, (((0,), (0,)), ((), ())), preferred_element_type=F32)


def bound_of(top_ref):
    return jnp.max(top_ref[...]) * 0.25 + EPS


def note_top(top_ref, step, values):
    largest = jnp.full(top_ref.shape, jnp.max(jnp.abs(values)), F32)

    @pl.when(step == 0)
    def _():
        top_ref[...] = largest

    @pl.when(step > 0)
    def _():
        top_ref[...] = jnp.maximum(top_ref[...], largest)


def halves(scal, width):
    part = width // 2
    near = scal[1]
    first = pl.ds(pl.multiple_of(near * part, part), part)
    second = pl.ds(pl.multiple_of((1 - near) * part, part), part)
    return first, second


def qkv_kernel(scal, x_ref, top_ref, own_ref, near_ref, far_ref, bown_ref, both_ref, a_ref, fac_ref, out_ref):
    bound = bound_of(top_ref)
    tangent = jnp.tanh(x_ref[...] * (1.0 / bound))
    low = (bound * tangent).astype(BF16)
    a_ref[...] = low
    fac_ref[...] = (1.0 - tangent * tangent).astype(BF16)
    first, second = halves(scal, low.shape[1])
    low_first, low_second = a_ref[:, first], a_ref[:, second]
    for j in range(3):
        own = nn(low, own_ref[0, j])
        oth = nn(low_first, near_ref[j]) + nn(low_second, far_ref[j])
        if j != 1:
            own = own + bown_ref[0, j // 2][None, :]
            oth = oth + both_ref[0, j // 2][None, :]
        out_ref[0, j] = own.astype(BF16)
        out_ref[1, j] = oth.astype(BF16)


def row_ids(scal, slots, half_rows):
    rows = 2 * half_rows
    slot = jnp.where(slots + half_rows * scal[2] >= rows, slots + half_rows * scal[2] - rows, slots + half_rows * scal[2])
    slot = slot + scal[0] * rows
    short = slot - LONG_DEV * LONG_LEN
    is_long = short < 0
    row = jnp.where(is_long, slot // LONG_LEN, LONG_DEV + short // SHORT_LEN)
    place = jnp.where(is_long, slot % LONG_LEN, short % SHORT_LEN)
    length = jnp.zeros_like(row)
    for i in range(LONG_DEV + SHORT_DEV):
        length = jnp.where(row == i, scal[3 + i], length)
    return row, place < length


HEADS = ((0, 128, 0), (0, 128, 1), (128, 192, None))


def lane_mask(rows, which):
    lane = lax.broadcasted_iota(jnp.int32, (rows, 128), 1)
    return (lane < HEAD_DIM) if which == 0 else (lane >= HEAD_DIM)


def only_head(values, which):
    if which is None:
        return values
    return jnp.where(lane_mask(values.shape[0], which), values, jnp.zeros_like(values))


def attend_kernel(scal, qkv_ref, ctx_ref, e_ref, rinv_ref, top_ref, bias_ref):
    step = pl.program_id(0)
    rows = qkv_ref.shape[2]

    @pl.when(step == 0)
    def _():
        q_row, _ = row_ids(scal, lax.broadcasted_iota(jnp.int32, (rows, 1), 0), rows // 2)
        k_row, k_live = row_ids(scal, lax.broadcasted_iota(jnp.int32, (1, rows), 1), rows // 2)
        k_row = jnp.where(k_live, k_row, -1)
        bias_ref[...] = jnp.where(q_row == k_row, 0.0, MASKED)

    scale = HEAD_DIM ** (-0.5)
    chunk = 128
    heads = []
    for h, (lo, hi, which) in enumerate(HEADS):
        keys = only_head(qkv_ref[0, 1, :, lo:hi], which)
        heads.append((h, lo, hi, which, keys, qkv_ref[0, 2, :, lo:hi]))
    for begin in range(0, rows, chunk):
        span = slice(begin, begin + chunk)
        done = []
        for h, lo, hi, which, keys, vals in heads:
            scores = nt(qkv_ref[0, 0, span, lo:hi], keys) * scale + bias_ref[span, :]
            weights = jnp.exp(scores - jnp.max(scores, axis=1, keepdims=True))
            inverse = 1.0 / jnp.sum(weights, axis=1, keepdims=True)
            low = weights.astype(BF16)
            e_ref[0, h, span, :] = low
            done.append((nn(low, vals) * inverse, inverse))
        left = lane_mask(chunk, 0)
        ctx_ref[0, span, 0:128] = jnp.where(left, done[0][0], done[1][0])
        ctx_ref[0, span, 128:192] = done[2][0]
        rinv_ref[0, span, 0:128] = jnp.where(left, done[0][1], done[1][1])
        rinv_ref[0, span, 128:192] = jnp.broadcast_to(done[2][1], (chunk, HEAD_DIM))
    note_top(top_ref, step, ctx_ref[...])


def out_kernel(scal, ctx_ref, top_ref, own_ref, near_ref, far_ref, c_ref, fac_ref, o_ref):
    bound = bound_of(top_ref)
    tangent = jnp.tanh(ctx_ref[...] * (1.0 / bound))
    c_ref[...] = (bound * tangent).astype(BF16)
    fac_ref[...] = (1.0 - tangent * tangent).astype(BF16)
    for part, ref in zip(halves(scal, o_ref.shape[1]), (near_ref, far_ref)):
        o_ref[:, part] = (nn(c_ref[0], own_ref[0, :, part]) + nn(c_ref[1], ref[...])).astype(BF16)


def norm_kernel(last, x_ref, self_ref, recv_ref, bias_ref, gain_ref, shift_ref, *outs):
    step = pl.program_id(0)
    branch = self_ref[...].astype(F32) + recv_ref[...].astype(F32) + bias_ref[...]
    mixed = x_ref[...].astype(F32) + branch
    centred = mixed - jnp.mean(mixed, axis=1, keepdims=True)
    inverse = lax.rsqrt(jnp.mean(centred * centred, axis=1, keepdims=True) + EPS)
    unit = centred * inverse
    result = unit * gain_ref[...] + shift_ref[...]
    h_ref, unit_ref, inv_ref, sums_ref = outs[:4]
    h_ref[...] = result.astype(h_ref.dtype)
    unit_ref[...] = unit
    inv_ref[...] = jnp.broadcast_to(inverse, inv_ref.shape)

    @pl.when(step == 0)
    def _():
        sums_ref[0:1, :] = jnp.full((1, 128), jnp.sum(branch * branch), F32)
        sums_ref[1:2, :] = jnp.full((1, 128), jnp.sum(result * result), F32)

    if not last:
        note_top(outs[4], step, result)


def up_kernel(scal, h_ref, top_ref, own_ref, near_ref, far_ref, bown_ref, both_ref, low_ref, fac_ref, g_ref, slope_ref, gtop_ref):
    step = pl.program_id(0)
    bound = bound_of(top_ref)
    tangent = jnp.tanh(h_ref[...] * (1.0 / bound))
    low = (bound * tangent).astype(BF16)
    low_ref[...] = low
    fac_ref[...] = (1.0 - tangent * tangent).astype(BF16)
    first, second = halves(scal, low.shape[1])
    for side in range(2):
        if side == 0:
            units = nn(low, own_ref[0]) + bown_ref[...]
        else:
            units = nn(low_ref[:, first], near_ref[...]) + nn(low_ref[:, second], far_ref[...]) + both_ref[...]
        area = 0.5 + 0.5 * lax.erf(units * (0.5**0.5))
        density = jnp.exp(-0.5 * units * units) * 0.3989422804014327
        g_ref[side] = units * area
        slope_ref[side] = (area + units * density).astype(BF16)
    note_top(gtop_ref, step, g_ref[...])


def down_kernel(scal, g_ref, slope_ref, top_ref, own_ref, near_ref, far_ref, low_ref, fac_ref, f_ref):
    bound = bound_of(top_ref)
    tangent = jnp.tanh(g_ref[...] * (1.0 / bound))
    low_ref[...] = (bound * tangent).astype(BF16)
    fac_ref[...] = ((1.0 - tangent * tangent) * slope_ref[...].astype(F32)).astype(BF16)
    first, second = halves(scal, g_ref.shape[2])
    f_ref[...] = (
        nn(low_ref[0], own_ref[0])
        + nn(low_ref[1, :, first], near_ref[...])
        + nn(low_ref[1, :, second], far_ref[...])
    ).astype(BF16)


def norm_back(grad, unit, inverse, gain):
    scaled = grad * gain
    return (
        scaled
        - jnp.mean(scaled, axis=1, keepdims=True)
        - unit * jnp.mean(scaled * unit, axis=1, keepdims=True)
    ) * inverse


def norm_sums(sums_ref, step, grad, unit, low):
    @pl.when(step == 0)
    def _():
        sums_ref[0:1, :] = jnp.sum(grad * unit, axis=0, keepdims=True)
        sums_ref[1:2, :] = jnp.sum(grad, axis=0, keepdims=True)
        sums_ref[2:3, :] = jnp.sum(low.astype(F32), axis=0, keepdims=True)


def ffn_back_kernel(from_input, scal, *refs):
    step = pl.program_id(0)
    if from_input:
        dy_ref, refs = refs[0], refs[1:]
        grad = dy_ref[...].astype(F32)
    else:
        (self_ref, recv_ref, infac_ref, skip_ref), refs = refs[:4], refs[4:]
        grad = (self_ref[...].astype(F32) + recv_ref[...].astype(F32)) * infac_ref[...].astype(F32) + skip_ref[...]
    (unit_ref, inv_ref, gain_ref, fac_ref, down_ref, dnear_ref, dfar_ref, up_ref, unear_ref, ufar_ref) = refs[:10]
    dz_ref, df_ref, du_ref, dh_ref, sums_ref, usum_ref = refs[10:]
    unit = unit_ref[...]
    mixed = norm_back(grad, unit, inv_ref[:, 0:1], gain_ref[...])
    low = mixed.astype(BF16)
    dz_ref[...] = mixed
    df_ref[...] = low
    norm_sums(sums_ref, step, grad, unit, low)
    first, second = halves(scal, low.shape[1])
    du_ref[0] = (nt(low, down_ref[0]) * fac_ref[0].astype(F32)).astype(BF16)
    for part, ref in ((first, dnear_ref), (second, dfar_ref)):
        du_ref[1, :, part] = (nt(low, ref[...]) * fac_ref[1, :, part].astype(F32)).astype(BF16)
    for part, ref in ((first, unear_ref), (second, ufar_ref)):
        dh_ref[:, part] = (nt(du_ref[0], up_ref[0, part, :]) + nt(du_ref[1], ref[...])).astype(BF16)
    for side in range(2):
        total = jnp.sum(du_ref[side].astype(F32), axis=0, keepdims=True)

        @pl.when(step == 0)
        def _():
            usum_ref[side : side + 1, :] = total

        @pl.when(step > 0)
        def _():
            usum_ref[side : side + 1, :] += total


def out_back_kernel(scal, self_ref, recv_ref, hfac_ref, skip_ref, unit_ref, inv_ref, gain_ref, cfac_ref, own_ref, near_ref, far_ref, dz_ref, do_ref, dctx_ref, sums_ref):
    step = pl.program_id(0)
    grad = (self_ref[...].astype(F32) + recv_ref[...].astype(F32)) * hfac_ref[...].astype(F32) + skip_ref[...]
    unit = unit_ref[...]
    mixed = norm_back(grad, unit, inv_ref[:, 0:1], gain_ref[...])
    low = mixed.astype(BF16)
    dz_ref[...] = mixed
    do_ref[...] = low
    norm_sums(sums_ref, step, grad, unit, low)
    first, second = halves(scal, low.shape[1])
    dctx_ref[0] = nt(low, own_ref[0]) * cfac_ref[0].astype(F32)
    oth = nt(do_ref[:, first], near_ref[...]) + nt(do_ref[:, second], far_ref[...])
    dctx_ref[1] = oth * cfac_ref[1].astype(F32)


def attend_back_kernel(qkv_ref, e_ref, rinv_ref, dctx_ref, ctx_ref, out_ref, sums_ref):
    rows = qkv_ref.shape[2]
    scale = HEAD_DIM ** (-0.5)
    low = (dctx_ref[0] * rinv_ref[0]).astype(BF16)
    product = low.astype(F32) * ctx_ref[0]
    results = []
    for h, (lo, hi, which) in enumerate(HEADS):
        inner = jnp.sum(only_head(product[:, lo:hi], which), axis=1, keepdims=True)
        values = only_head(qkv_ref[0, 2, :, lo:hi], which)
        weights = e_ref[0, h]
        grad_weights = nt(low[:, lo:hi], values)
        grad_scores = (weights.astype(F32) * (grad_weights - inner)).astype(BF16)
        dq = nn(grad_scores, qkv_ref[0, 1, :, lo:hi]) * scale
        dk = tn(grad_scores, qkv_ref[0, 0, :, lo:hi]) * scale
        dv = tn(weights, low[:, lo:hi])
        results.append((dq, dk, dv))
    left = lane_mask(rows, 0)
    for j in range(3):
        pair = jnp.where(left, results[0][j], results[1][j]).astype(BF16)
        last = results[2][j].astype(BF16)
        out_ref[0, j, :, 0:128] = pair
        out_ref[0, j, :, 128:192] = last
        if j != 1:
            place = slice(j // 2, j // 2 + 1)
            sums_ref[0, place, 0:128] = jnp.sum(pair.astype(F32), axis=0, keepdims=True)
            sums_ref[0, place, 128:192] = jnp.sum(last.astype(F32), axis=0, keepdims=True)


def qkv_back_kernel(scal, d_ref, own_ref, near_ref, far_ref, da_ref):
    for part, ref in zip(halves(scal, da_ref.shape[1]), (near_ref, far_ref)):
        total = nt(d_ref[0, 0], own_ref[0, 0, part, :]) + nt(d_ref[1, 0], ref[0])
        for j in (1, 2):
            total = total + nt(d_ref[0, j], own_ref[0, j, part, :]) + nt(d_ref[1, j], ref[j])
        da_ref[:, part] = total.astype(BF16)


def ffn_grad_kernel(df_ref, gq_ref, hq_ref, du_ref, down_own, down_oth, up_own, up_oth):
    down_own[...] = tn(df_ref[...], gq_ref[0])
    down_oth[...] = tn(df_ref[...], gq_ref[1]).astype(BF16)
    up_own[...] = tn(hq_ref[...], du_ref[0])
    up_oth[...] = tn(hq_ref[...], du_ref[1]).astype(BF16)


def attn_grad_kernel(a_ref, d_ref, do_ref, c_ref, own_a, oth_a, own_b, oth_b):
    for j in range(2):
        own_a[j] = tn(a_ref[...], d_ref[0, j])
        oth_a[j] = tn(a_ref[...], d_ref[1, j]).astype(BF16)
    own_b[0] = tn(a_ref[...], d_ref[0, 2])
    oth_b[0] = tn(a_ref[...], d_ref[1, 2]).astype(BF16)
    own_b[1] = tn(do_ref[...], c_ref[0])
    oth_b[1] = tn(do_ref[...], c_ref[1]).astype(BF16)


def spec(shape, index):
    return pl.BlockSpec(shape, index)


def whole(array):
    dims = len(array.shape)
    return pl.BlockSpec(array.shape, lambda i: (0,) * dims)


def layer_block(array, layer):
    dims = len(array.shape)
    return pl.BlockSpec((1,) + array.shape[1:], lambda i: (layer,) + (0,) * (dims - 1))


SCALARS = pl.BlockSpec(memory_space=pltpu.SMEM)


def run(kernel, steps, ins, outs, name, flops=0, scratch=()):
    arrays = [array for array, _ in ins]
    moved = sum(a.size * a.dtype.itemsize for a in arrays) + sum(
        jax.ShapeDtypeStruct(s, d).size * jnp.dtype(d).itemsize for s, d, _ in outs
    )
    return pl.pallas_call(
        kernel,
        grid=(steps,),
        in_specs=[s for _, s in ins],
        out_specs=[s for _, _, s in outs],
        out_shape=[jax.ShapeDtypeStruct(s, d) for s, d, _ in outs],
        scratch_shapes=list(scratch),
        name=name,
        cost_estimate=pl.CostEstimate(flops=int(flops), bytes_accessed=int(moved), transcendentals=0),
        compiler_params=pltpu.CompilerParams(vmem_limit_bytes=VMEM_LIMIT),
    )(*arrays)


def body(
    hidden,
    long_lengths,
    short_lengths,
    w_qkv,
    bias_qv,
    w_out,
    bias_out,
    ln_gain,
    ln_bias,
    w_up,
    bias_up,
    w_down,
    bias_down,
    cotangent,
):
    own_rows, width = hidden.shape
    rows = 2 * own_rows
    heads_width = w_qkv.shape[-1]
    units = w_up.shape[-1]
    dp_size, tensor_size = lax.axis_size("dp"), lax.axis_size("tensor")
    devices = dp_size * tensor_size
    count_model = float(own_rows * devices * width)
    dp_index, tensor_index = lax.axis_index("dp"), lax.axis_index("tensor")
    x_index, core_index, y_index = tensor_index // 2, tensor_index % 2, dp_index % 2
    core_pairs = [(i, i ^ 1) for i in range(tensor_size)]
    x_pairs = [(i, i ^ 2) for i in range(tensor_size)]
    dp_pairs = lambda bit: [(i, i ^ bit) for i in range(dp_size)]
    core_swap = lambda v: lax.ppermute(v, "tensor", core_pairs)
    x_swap = lambda v: lax.ppermute(v, "tensor", x_pairs)
    dp_swap = lambda v, bit: lax.ppermute(v, "dp", dp_pairs(bit))

    scal = jnp.concatenate(
        [jnp.stack([x_index, y_index, core_index]).astype(jnp.int32), long_lengths, short_lengths]
    )
    blk = own_rows
    steps = 2

    def over_ranks(top):
        return lax.all_to_all(top, BOTH, 0, 0)

    def relay(values, axis):
        part = values.shape[axis] // 2
        near = x_swap(lax.dynamic_slice_in_dim(values, y_index * part, part, axis))
        return near, dp_swap(near, 1)

    row_block = lambda a: (a, spec((blk,) + a.shape[1:], lambda i: (i, 0)))
    swapped = lambda a: (a, spec((blk,) + a.shape[1:], lambda i: (1 - i, 0)))
    side_block = lambda a: (a, spec((2, blk, a.shape[2]), lambda i: (0, i, 0)))
    full = lambda a: (a, whole(a))
    scalars = (scal, SCALARS)
    out_rows = lambda w, d: ((rows, w), d, spec((blk, w), lambda i: (i, 0)))
    out_sides = lambda w, d: ((2, rows, w), d, spec((2, blk, w), lambda i: (0, i, 0)))
    fixed = lambda s, d: (s, d, spec(s, lambda i: (0,) * len(s)))
    top_shape = (devices, 1, 128)

    hidden_full = jnp.concatenate([hidden, core_swap(hidden)], 0)

    def top_kernel(x_ref, top_ref, sums_ref):
        values = x_ref[...].astype(F32)
        note_top(top_ref, pl.program_id(0), values)
        sums_ref[...] = jnp.full((1, 128), jnp.sum(values * values), F32)

    top, input_sum = run(
        top_kernel, 1, [full(hidden)], [fixed(top_shape, F32), fixed((1, 128), F32)], "input_top"
    )
    top = over_ranks(top)
    states = hidden_full.astype(F32)

    small = jnp.concatenate([bias_qv.reshape(LAYERS, 2 * heads_width), bias_up], 1)
    small = x_swap(small)
    oth_bias_qv = small[:, : 2 * heads_width].reshape(LAYERS, 2, heads_width)
    oth_bias_up = small[:, 2 * heads_width :]
    saved = []
    square_terms = []
    for l in range(LAYERS):
        last = l == LAYERS - 1
        qkv_near, qkv_far = relay(w_qkv[l], 1)
        out_near, out_far = relay(w_out[l], 1)
        up_near, up_far = relay(w_up[l], 0)
        down_near, down_far = relay(w_down[l], 0)
        low_in, fac_in, qkv = run(
            qkv_kernel,
            steps,
            [scalars, row_block(states), full(top), (w_qkv, layer_block(w_qkv, l)), full(qkv_near), full(qkv_far),
             (bias_qv, layer_block(bias_qv, l)), (oth_bias_qv, layer_block(oth_bias_qv, l))],
            [out_rows(width, BF16), out_rows(width, BF16),
             ((2, 3, rows, heads_width), BF16, spec((2, 3, blk, heads_width), lambda i: (0, 0, i, 0)))],
            "qkv",
            flops=2 * rows * width * heads_width * 6,
        )
        ctx, weights, rinv, top = run(
            attend_kernel,
            2,
            [scalars, (qkv, spec((1, 3, rows, heads_width), lambda i: (i, 0, 0, 0)))],
            [((2, rows, heads_width), F32, spec((1, rows, heads_width), lambda i: (i, 0, 0))),
             ((2, 3, rows, rows), BF16, spec((1, 3, rows, rows), lambda i: (i, 0, 0, 0))),
             ((2, rows, heads_width), F32, spec((1, rows, heads_width), lambda i: (i, 0, 0))),
             fixed(top_shape, F32)],
            "attend",
            flops=12 * rows * rows * 128 * 8,
            scratch=[pltpu.VMEM((rows, rows), F32)],
        )
        top = over_ranks(top)
        low_ctx, fac_ctx, part = run(
            out_kernel,
            steps,
            [scalars, side_block(ctx), full(top), (w_out, layer_block(w_out, l)), full(out_near), full(out_far)],
            [out_sides(heads_width, BF16), out_sides(heads_width, BF16), out_rows(width, BF16)],
            "out_proj",
            flops=4 * rows * width * heads_width,
        )
        gain = ln_gain[l]
        shift = ln_bias[l]
        row_vec = lambda v: full(v.reshape(1, -1))
        middle, unit_one, inv_one, sums_one, top = run(
            partial(norm_kernel, False),
            steps,
            [row_block(states), row_block(part), swapped(core_swap(part)), row_vec(bias_out[l]), row_vec(gain[0]), row_vec(shift[0])],
            [out_rows(width, F32), out_rows(width, F32), out_rows(128, F32), fixed((2, 128), F32), fixed(top_shape, F32)],
            "norm_one",
        )
        top = over_ranks(top)
        low_mid, fac_mid, active, slope, top = run(
            up_kernel,
            steps,
            [scalars, row_block(middle), full(top), (w_up, layer_block(w_up, l)), full(up_near), full(up_far),
             row_vec(bias_up[l]), row_vec(oth_bias_up[l])],
            [out_rows(width, BF16), out_rows(width, BF16), out_sides(units, F32), out_sides(units, BF16), fixed(top_shape, F32)],
            "up_proj",
            flops=4 * rows * width * units,
        )
        top = over_ranks(top)
        low_act, fac_act, part = run(
            down_kernel,
            steps,
            [scalars, side_block(active), side_block(slope), full(top), (w_down, layer_block(w_down, l)), full(down_near), full(down_far)],
            [out_sides(units, BF16), out_sides(units, BF16), out_rows(width, BF16)],
            "down_proj",
            flops=4 * rows * width * units,
        )
        outs = run(
            partial(norm_kernel, last),
            steps,
            [row_block(middle), row_block(part), swapped(core_swap(part)), row_vec(bias_down[l]), row_vec(gain[1]), row_vec(shift[1])],
            [out_rows(width, BF16 if last else F32), out_rows(width, F32), out_rows(128, F32), fixed((2, 128), F32)]
            + ([] if last else [fixed(top_shape, F32)]),
            "norm_two",
        )
        unit_two, inv_two, sums_two = outs[1:4]
        square_terms += [input_sum[0, 0], sums_one[0, 0], sums_two[0, 0]]
        input_sum = sums_two[1:2]
        saved.append(
            (low_in, fac_in, qkv, ctx, weights, rinv, low_ctx, fac_ctx, unit_one, inv_one, low_mid, fac_mid,
             low_act, fac_act, unit_two, inv_two, gain, qkv_near, qkv_far, out_near, out_far, up_near, up_far, down_near, down_far)
        )
        states = outs[0]
        if not last:
            top = over_ranks(outs[4])
    output = states[:own_rows]

    cot_full = jnp.concatenate([cotangent, core_swap(cotangent)], 0)

    def take(values, index):
        return lax.dynamic_index_in_dim(values, index, 2, keepdims=False)

    def fold_dp(total, begin_bit):
        bit = begin_bit
        while bit < dp_size:
            mine = (dp_index // bit) % 2
            shape = total.shape
            view = total.reshape(shape[0], shape[1] // 2, 2, *shape[2:])
            total = take(view, mine) + dp_swap(take(view, 1 - mine).astype(BF16), bit).astype(F32)
            bit *= 2
        return total[:, 0]

    def by_slices(values):
        return values.reshape(values.shape[0], dp_size, values.shape[1] // dp_size, values.shape[2])

    def reduce_x_first(own, oth):
        total = own + x_swap(oth).astype(F32)
        return fold_dp(by_slices(total), 1)

    def reduce_y_first(own, oth):
        mine = y_index
        own, oth = by_slices(own), by_slices(oth)
        pair = lambda v: v.reshape(v.shape[0], dp_size // 2, 2, *v.shape[2:])
        own, oth = pair(own), pair(oth)
        away = jnp.stack([take(own, 1 - mine).astype(BF16), take(oth, 1 - mine)])
        got = dp_swap(away, 1).astype(F32)
        other = (take(oth, mine).astype(F32) + got[1]).astype(BF16)
        total = take(own, mine) + got[0] + x_swap(other).astype(F32)
        return fold_dp(total, 2)

    grads = [None] * LAYERS
    sums = [None] * LAYERS
    grad_source = None
    for l in reversed(range(LAYERS)):
        (low_in, fac_in, qkv, ctx, weights, rinv, low_ctx, fac_ctx, unit_one, inv_one, low_mid, fac_mid,
         low_act, fac_act, unit_two, inv_two, gain, qkv_near, qkv_far, out_near, out_far, up_near, up_far, down_near, down_far) = saved[l]
        if grad_source is None:
            first_ins = [row_block(cot_full)]
        else:
            part, fac, skip = grad_source
            first_ins = [row_block(part), swapped(core_swap(part)), row_block(fac), row_block(skip)]
        dz_two, df, du, part, sums_two, unit_sums = run(
            partial(ffn_back_kernel, grad_source is None),
            steps,
            [scalars] + first_ins
            + [row_block(unit_two), row_block(inv_two), row_vec(gain[1]), side_block(fac_act),
               (w_down, layer_block(w_down, l)), full(down_near), full(down_far),
               (w_up, layer_block(w_up, l)), full(up_near), full(up_far)],
            [out_rows(width, F32), out_rows(width, BF16), out_sides(units, BF16), out_rows(width, BF16),
             fixed((3, width), F32), fixed((2, units), F32)],
            "ffn_back",
            flops=8 * rows * width * units,
        )
        down_own, down_oth, up_own, up_oth = run(
            ffn_grad_kernel,
            1,
            [full(df), full(low_act), full(low_mid), full(du)],
            [fixed((width, units), F32), fixed((width, units), BF16), fixed((width, units), F32), fixed((width, units), BF16)],
            "ffn_grad",
            flops=8 * rows * width * units,
        )
        dz_one, do, dctx, sums_one = run(
            out_back_kernel,
            steps,
            [scalars, row_block(part), swapped(core_swap(part)), row_block(fac_mid), row_block(dz_two), row_block(unit_one),
             row_block(inv_one), row_vec(gain[0]), side_block(fac_ctx), (w_out, layer_block(w_out, l)), full(out_near), full(out_far)],
            [out_rows(width, F32), out_rows(width, BF16), out_sides(heads_width, F32), fixed((3, width), F32)],
            "out_back",
            flops=4 * rows * width * heads_width,
        )
        per_side = lambda a: (a, spec((1,) + a.shape[1:], lambda i: (i,) + (0,) * (len(a.shape) - 1)))
        dqkv, head_sums = run(
            attend_back_kernel,
            2,
            [per_side(qkv), per_side(weights), per_side(rinv), per_side(dctx), per_side(ctx)],
            [((2, 3, rows, heads_width), BF16, spec((1, 3, rows, heads_width), lambda i: (i, 0, 0, 0))),
             ((2, 2, heads_width), F32, spec((1, 2, heads_width), lambda i: (i, 0, 0)))],
            "attend_back",
            flops=6 * rows * rows * 128 * 8,
        )
        (part,) = run(
            qkv_back_kernel,
            steps,
            [scalars, (dqkv, spec((2, 3, blk, heads_width), lambda i: (0, 0, i, 0))), (w_qkv, layer_block(w_qkv, l)), full(qkv_near), full(qkv_far)],
            [out_rows(width, BF16)],
            "qkv_back",
            flops=2 * rows * width * heads_width * 6,
        )
        own_a, oth_a, own_b, oth_b = run(
            attn_grad_kernel,
            1,
            [full(low_in), full(dqkv), full(do), full(low_ctx)],
            [fixed((2, width, heads_width), F32), fixed((2, width, heads_width), BF16)] * 2,
            "attn_grad",
            flops=2 * rows * width * heads_width * 8,
        )
        grad_source = (part, fac_in, dz_one)
        grads[l] = (
            reduce_x_first(up_own[None], up_oth[None])[0],
            reduce_y_first(down_own[None], down_oth[None])[0],
            reduce_x_first(own_a, oth_a),
            reduce_y_first(own_b, oth_b),
        )
        sums[l] = (sums_one, sums_two, head_sums, unit_sums)
    part, fac, skip = grad_source
    grad_hidden = (
        part[:own_rows].astype(F32) + core_swap(part[own_rows:]).astype(F32)
    ) * fac[:own_rows].astype(F32) + skip[:own_rows]

    oth_index = tensor_index ^ 2
    pieces = []
    for l in range(LAYERS):
        sums_one, sums_two, head_sums, unit_sums = sums[l]
        pieces += [sums_one.reshape(-1), sums_two.reshape(-1)]
        for values in (head_sums.reshape(2, -1), unit_sums):
            spread = jnp.zeros((tensor_size, values.shape[1]), F32)
            spread = lax.dynamic_update_slice_in_dim(spread, values[0:1], tensor_index, 0)
            spread = lax.dynamic_update_slice_in_dim(spread, values[1:2], oth_index, 0)
            pieces.append(spread.reshape(-1))
    pieces.append(jnp.stack(square_terms))
    flat = jnp.concatenate(pieces)
    chunk = -(-flat.shape[0] // (devices * 128)) * 128
    flat = jnp.pad(flat, (0, devices * chunk - flat.shape[0])).reshape(devices, 1, chunk)
    mine = jnp.sum(lax.all_to_all(flat, BOTH, 0, 0), axis=0, keepdims=True)
    totals = lax.all_to_all(jnp.broadcast_to(mine, flat.shape), BOTH, 0, 0).reshape(-1)
    offset = 0

    def next_piece(shape):
        nonlocal offset
        size = 1
        for n in shape:
            size *= n
        value = totals[offset : offset + size].reshape(shape)
        offset += size
        return value

    gains, shifts, out_biases, down_biases, head_biases, unit_biases = [], [], [], [], [], []
    own_shard = lambda v: lax.dynamic_index_in_dim(v, tensor_index, 0, keepdims=False)
    for l in range(LAYERS):
        one = next_piece((3, width))
        two = next_piece((3, width))
        gains.append(jnp.stack([one[0], two[0]]))
        shifts.append(jnp.stack([one[1], two[1]]))
        out_biases.append(one[2])
        down_biases.append(two[2])
        head_biases.append(own_shard(next_piece((tensor_size, 2, heads_width))))
        unit_biases.append(own_shard(next_piece((tensor_size, units))))
    rms_values = jnp.sqrt(next_piece((LAYERS, 3)) / count_model)
    return (
        output,
        grad_hidden,
        jnp.stack([jnp.concatenate([g[2], g[3][0:1]], 0) for g in grads]),
        jnp.stack(head_biases),
        jnp.stack([g[3][1].T for g in grads]),
        jnp.stack(out_biases),
        jnp.stack(gains),
        jnp.stack(shifts),
        jnp.stack([g[0] for g in grads]),
        jnp.stack(unit_biases),
        jnp.stack([g[1].T for g in grads]),
        jnp.stack(down_biases),
        rms_values,
    )


def solution(mesh):
    in_specs = (
        P(("dp", "tensor"), None),
        P("dp"),
        P("dp"),
        P(None, None, None, "tensor"),
        P(None, None, "tensor"),
        P(None, "tensor", None),
        P(),
        P(),
        P(),
        P(None, None, "tensor"),
        P(None, "tensor"),
        P(None, "tensor", None),
        P(),
        P(("dp", "tensor"), None),
    )
    out_specs = (
        P(("dp", "tensor"), None),
        P(("dp", "tensor"), None),
        P(None, None, "dp", "tensor"),
        P(None, None, "tensor"),
        P(None, "tensor", "dp"),
        P(),
        P(),
        P(),
        P(None, "dp", "tensor"),
        P(None, "tensor"),
        P(None, "tensor", "dp"),
        P(),
        P(),
    )
    return jax.shard_map(body, mesh=mesh, in_specs=in_specs, out_specs=out_specs, check_vma=False)
```

time: 1350 us -> 595 us (0.44)
  waiting for transfers between devices: 682 us -> 143 us
  blocking collectives: 396 us -> 0 us
  local copies, waits for them, and re-layouts: 60.3 us -> 192 us
  matrix products: 110 us -> 0 us
  Pallas kernels: 0 us -> 104 us
  starting transfers between devices: 1.85 us -> 98.1 us
  other arithmetic: 66.5 us -> 44.6 us
  between operations: 23.7 us -> 3.64 us
    reduce_scatter x9 -> x0, waiting for transfers between devices: 362 us -> none  [the longest x4 153 us: forward_rows(): lax.psum_scatter(row_term(jnp.int32(0), row_count * lax.axis_size('tensor...]
    pmax x8 -> x0, blocking collectives: 319 us -> none  [global_top(): return lax.pmax(jnp.max(jnp.abs(values)), ('dp', 'tensor'))]
    unnamed x23 -> x0, waiting for transfers between devices: 184 us -> none
    all_gather x8 -> x0, waiting for transfers between devices: 136 us -> none  [the longest x4 77.2 us: gather_inputs(): return lax.all_gather(values, 'tensor', axis=0, tiled=True)]
    dot_general x46 -> x0, matrix products: 105 us -> none  [the longest x2 24.6 us: body(): jnp.dot(gathered_mid, w_up[layer_index], preferred_element_type=jnp.float32)]
    pallas_call x0 -> x27, Pallas kernels: none -> 104 us  [run(): pl.pallas_call(kernel, grid=(steps,), in_specs=[s for _, s in ins], out_s...]
    ppermute x0 -> x59, waiting for transfers between devices: none -> 97.2 us  [the longest x32 72.1 us: body(): dp_swap = lambda v, bit: lax.ppermute(v, 'dp', dp_pairs(bit))]
    psum x2 -> x0, blocking collectives: 76.8 us -> none  [the longest x1 41.6 us: body(): lax.psum((jnp.stack(out_bias_list), jnp.stack(down_bias_list), jnp.stack(...]
  transfers between devices with their start and end apart: 20 -> 69, of which waited for: 20 -> 27; matrix products, arithmetic and copies ran while one was open for 7% -> 22% of each run, Pallas kernels for 0% -> 15%
where the time goes in v1:
time: 595 us; the launch traced here: 584 us
  local copies, waits for them, and re-layouts  192 us (32%)
  waiting for transfers between devices  143 us (24%)
  Pallas kernels  104 us (17%)
  starting transfers between devices  98.1 us (16%)
  other arithmetic  44.6 us (7%)
    unnamed x402, local copies, waits for them, and re-layouts  110 us
    pallas_call x27, Pallas kernels, run(): pl.pallas_call(kernel, grid=(steps,), in_specs=[s for _, s in ins], out_s...  104 us
    ppermute x32, waiting for transfers between devices, body(): dp_swap = lambda v, bit: lax.ppermute(v, 'dp', dp_pairs(bit))  72.1 us
    all_to_all x8, waiting for transfers between devices, over_ranks(): return lax.all_to_all(top, BOTH, 0, 0)  43.4 us
    all_to_all x8, starting transfers between devices, over_ranks(): return lax.all_to_all(top, BOTH, 0, 0)  34.5 us
    ppermute x32, starting transfers between devices, body(): dp_swap = lambda v, bit: lax.ppermute(v, 'dp', dp_pairs(bit))  33.7 us
    ppermute x17, waiting for transfers between devices, body(): x_swap = lambda v: lax.ppermute(v, 'tensor', x_pairs)  22.5 us
    ppermute x17, starting transfers between devices, body(): x_swap = lambda v: lax.ppermute(v, 'tensor', x_pairs)  18.4 us
  transfers between devices with their start and end apart: 69, of which 27 were waited for; matrix products, arithmetic and copies ran while one was open for 22% of the time, Pallas kernels for 15%

profile of v1, /device:TPU:0, one launch (start us, length us, event | category | flops | bytes accessed | tf_op | source)
XLA Modules:
  0.0 584.3 jit_solution(8405512103138972159)
XLA Ops:
  3.0 7.1 %all-to-all-start = ((f32[32,1,128]{2,1,0:T(1,128)}), f32[32,1,128]{2,1,0:T(1,128)}, u32[]{:S(2)}, u32[]{:S(2)}) async-start(f32[32,1,128]{2,1,0:T(1,128)} %get-tuple-element.110), calls=%async_computation | async-start | bytes 32768 | tf_op jit(solution)/shard_map/all_to_all | solution.py:399
  22.1 6.2 %collective-permute-done.1 = bf16[3,384,192]{1,2,0:T(8,128)(2,1)} collective-permute-done((bf16[3,384,192]{1,2,0:T(8,128)(2,1)}, bf16[3,384,192]{1,2,0:T(8,128)(2,1)}, u32[]{:S(2)}, u32[]{:S(2)}) %collective-permute-start.1) | collective-permute-done | bytes 442400 | tf_op jit(solution)/shard_map/ppermute | solution.py:389
  52.3 8.0 %attend.2 = (f32[2,512,192]{2,1,0:T(8,128)S(1)}, bf16[2,3,512,512]{3,2,1,0:T(8,128)(2,1)S(1)}, f32[2,512,192]{2,1,0:T(8,128)S(1)}, f32[32,1,128]{2,1,0:T(1,128)S(1)}) custom-call(s32[8]{0:T(128)S(1)} %concatenate.22.scal, bf16[2,3,512,192]{3,2,1,0:T(8,128)(2,1)S(1)} %get-tuple-element.111.qkv_ref), custom_call_target="tpu_custom_call" | custom-call | flops 3221225472 | bytes 5914656 | tf_op jit(solution)/shard_map/attend/pallas_call | solution.py:347
  64.5 5.9 %all-to-all-start.1 = ((f32[32,1,128]{2,1,0:T(1,128)}), f32[32,1,128]{2,1,0:T(1,128)}, u32[]{:S(2)}, u32[]{:S(2)}) async-start(f32[32,1,128]{2,1,0:T(1,128)} %copy-done.129), calls=%async_computation.1 | async-start | bytes 32768 | tf_op jit(solution)/shard_map/all_to_all | solution.py:399
  96.8 4.7 all-to-all-start.2
  102.9 9.9 %all-to-all-done.2.top_ref = f32[32,1,128]{2,1,0:T(1,128)} async-done(((f32[32,1,128]{2,1,0:T(1,128)}), f32[32,1,128]{2,1,0:T(1,128)}, u32[]{:S(2)}, u32[]{:S(2)}) %all-to-all-start.2) | async-done | bytes 16416 | tf_op jit(solution)/shard_map/all_to_all | solution.py:399
  141.2 5.3 down_proj.2
  180.2 8.0 %attend.3 = (f32[2,512,192]{2,1,0:T(8,128)S(1)}, bf16[2,3,512,512]{3,2,1,0:T(8,128)(2,1)S(1)}, f32[2,512,192]{2,1,0:T(8,128)S(1)}, f32[32,1,128]{2,1,0:T(1,128)S(1)}) custom-call(s32[8]{0:T(128)S(1)} %concatenate.22.scal, bf16[2,3,512,192]{3,2,1,0:T(8,128)(2,1)S(1)} %get-tuple-element.123.qkv_ref), custom_call_target="tpu_custom_call" | custom-call | flops 3221225472 | bytes 5914656 | tf_op jit(solution)/shard_map/attend/pallas_call | solution.py:347
  196.5 7.0 %all-to-all-done.5.top_ref = f32[32,1,128]{2,1,0:T(1,128)} async-done(((f32[32,1,128]{2,1,0:T(1,128)}), f32[32,1,128]{2,1,0:T(1,128)}, u32[]{:S(2)}, u32[]{:S(2)}) %all-to-all-start.5) | async-done | bytes 16416 | tf_op jit(solution)/shard_map/all_to_all | solution.py:399
  225.4 12.4 %all-to-all-done.6.top_ref = f32[32,1,128]{2,1,0:T(1,128)} async-done(((f32[32,1,128]{2,1,0:T(1,128)}), f32[32,1,128]{2,1,0:T(1,128)}, u32[]{:S(2)}, u32[]{:S(2)}) %all-to-all-start.6) | async-done | bytes 16416 | tf_op jit(solution)/shard_map/all_to_all | solution.py:399
  253.1 7.1 %all-to-all-done.7.top_ref = f32[32,1,128]{2,1,0:T(1,128)S(1)} async-done(((f32[32,1,128]{2,1,0:T(1,128)}), f32[32,1,128]{2,1,0:T(1,128)S(1)}, u32[]{:S(2)}, u32[]{:S(2)}) %all-to-all-start.7) | async-done | bytes 16416 | tf_op jit(solution)/shard_map/all_to_all | solution.py:399
  265.2 5.1 down_proj.3
  282.9 7.5 %ffn_back.2 = (f32[512,768]{1,0:T(8,128)S(1)}, bf16[512,768]{1,0:T(8,128)(2,1)S(1)}, bf16[2,512,768]{2,1,0:T(8,128)(2,1)S(1)}, bf16[512,768]{1,0:T(8,128)(2,1)S(...) custom-call(s32[8]{0:T(128)S(1)} %concatenate.22.scal, bf16[512,768]{1,0:T(8,128)(2,1)S(1)} %pad_maximum_fusion.2.refs_0_, ...), custom_call_target="tpu_custom_call" | custom-call | flops 2415919104 | bytes 16009248 | tf_op jit(solution)/shard_map/ffn_back/pallas_call | solution.py:347
  344.3 12.5 %collective-permute-done.39 = bf16[2,2,4,96,192]{4,3,2,1,0:T(8,128)(2,1)} collective-permute-done((bf16[2,2,4,96,192]{4,3,2,1,0:T(8,128)(2,1)}, bf16[2,2,4,96,192]{4,3,2,1,0:T(8,128)(2,1)}, u32[]{:S(2)}, u32[]{:S(2)}) %collective-permute-start.39) | collective-permute-done | bytes 589856 | tf_op jit(solution)/shard_map/ppermute | solution.py:390
  368.7 9.0 %ffn_back.3 = (f32[512,768]{1,0:T(8,128)S(1)}, bf16[512,768]{1,0:T(8,128)(2,1)S(1)}, bf16[2,512,768]{2,1,0:T(8,128)(2,1)S(1)}, bf16[512,768]{1,0:T(8,128)(2,1)},...) custom-call(s32[8]{0:T(128)S(1)} %concatenate.22.scal, bf16[512,768]{1,0:T(8,128)(2,1)} %qkv_back.2.refs_0_, ...), custom_call_target="tpu_custom_call" | custom-call | flops 2415919104 | bytes 19154976 | tf_op jit(solution)/shard_map/ffn_back/pallas_call | solution.py:347
  410.1 5.4 collective-permute-done.42
  425.3 7.7 %collective-permute-done.57 = bf16[1,2,96,768]{3,2,1,0:T(8,128)(2,1)S(1)} collective-permute-done((bf16[1,2,96,768]{3,2,1,0:T(8,128)(2,1)S(1)}, bf16[1,2,96,768]{3,2,1,0:T(8,128)(2,1)S(1)}, u32[]{:S(2)}, u32[]{:S(2)}) %collective-permute-start.57) | collective-permute-done | bytes 294944 | tf_op jit(solution)/shard_map/ppermute | solution.py:390
  435.0 4.8 collective-permute-done.58
  467.9 4.8 concatenate.27
  489.4 5.9 %all-to-all-start.9 = ((f32[32,1,640]{2,1,0:T(1,128)}), f32[32,1,640]{2,1,0:T(1,128)}, u32[]{:S(2)}, u32[]{:S(2)}) async-start(f32[32,1,640]{2,1,0:T(1,128)} %broadcast_in_dim.18), calls=%async_computation.9 | async-start | bytes 163840 | tf_op jit(solution)/shard_map/all_to_all | solution.py:648
  525.3 14.0 %collective-permute-done.32 = bf16[2,4,96,192]{3,2,1,0:T(8,128)(2,1)} collective-permute-done((bf16[2,4,96,192]{3,2,1,0:T(8,128)(2,1)S(1)}, bf16[2,4,96,192]{3,2,1,0:T(8,128)(2,1)}, u32[]{:S(2)}, u32[]{:S(2)}) %collective-permute-start.32) | collective-permute-done | bytes 294944 | tf_op jit(solution)/shard_map/ppermute | solution.py:389
  549.3 6.6 %collective-permute-done.29 = bf16[2,2,96,192]{3,2,1,0:T(8,128)(2,1)S(1)} collective-permute-done((bf16[2,2,96,192]{3,2,1,0:T(8,128)(2,1)S(1)}, bf16[2,2,96,192]{3,2,1,0:T(8,128)(2,1)S(1)}, u32[]{:S(2)}, u32[]{:S(2)}) %collective-permute-start.29) | collective-permute-done | bytes 147488 | tf_op jit(solution)/shard_map/ppermute | solution.py:390
  556.1 8.4 %collective-permute-done.34 = bf16[2,1,96,192]{3,2,1,0:T(8,128)(2,1)S(1)} collective-permute-done((bf16[2,1,96,192]{3,2,1,0:T(8,128)(2,1)S(1)}, bf16[2,1,96,192]{3,2,1,0:T(8,128)(2,1)S(1)}, u32[]{:S(2)}, u32[]{:S(2)}) %collective-permute-start.34) | collective-permute-done | bytes 73760 | tf_op jit(solution)/shard_map/ppermute | solution.py:390
  573.0 8.2 %collective-permute-done.46 = bf16[1,1,96,768]{3,2,1,0:T(8,128)(2,1)S(1)} collective-permute-done((bf16[1,1,96,768]{3,2,1,0:T(8,128)(2,1)S(1)}, bf16[1,1,96,768]{3,2,1,0:T(8,128)(2,1)S(1)}, u32[]{:S(2)}, u32[]{:S(2)}) %collective-permute-start.46) | collective-permute-done | bytes 147488 | tf_op jit(solution)/shard_map/ppermute | solution.py:390
  (717 shorter events, 399.3 us)
Async XLA Ops:
  0.6 36.2 %collective-permute-start = (bf16[256,768]{1,0:T(8,128)(2,1)}, bf16[256,768]{1,0:T(8,128)(2,1)}, u32[]{:S(2)}, u32[]{:S(2)}) collective-permute-start(bf16[256,768]{1,0:T(8,128)(2,1)} %x_ref.1), channel_id=1, source_target_pairs={{0,1},{1,0},{2,3},{3,2},{4,5},{5,4},{6,7},{7,6},{8,9},{9,8},{10,11... | collective-permute-start | bytes 1179656 | tf_op jit(solution)/shard_map/ppermute | solution.py:388
  3.0 39.9 %all-to-all-start = ((f32[32,1,128]{2,1,0:T(1,128)}), f32[32,1,128]{2,1,0:T(1,128)}, u32[]{:S(2)}, u32[]{:S(2)}) async-start(f32[32,1,128]{2,1,0:T(1,128)} %get-tuple-element.110), calls=%async_computation | async-start | bytes 32768 | tf_op jit(solution)/shard_map/all_to_all | solution.py:399
  21.8 62.1 %collective-permute-start.7 = (bf16[384,768]{1,0:T(8,128)(2,1)}, bf16[384,768]{1,0:T(8,128)(2,1)}, u32[]{:S(2)}, u32[]{:S(2)}) collective-permute-start(bf16[384,768]{1,0:T(8,128)(2,1)} %dynamic-slice_bitcast_fusion.5), channel_id=1, source_target_pairs={{0,2},{1,3},{2,0},{3,1},{4,6},{5,7},{6,4},{7,5},{8,10},{9,11},{10,... | collective-permute-start | bytes 1769480 | tf_op jit(solution)/shard_map/ppermute | solution.py:389
  36.5 37.4 %collective-permute-start.5 = (bf16[192,384]{1,0:T(8,128)(2,1)}, bf16[192,384]{1,0:T(8,128)(2,1)}, u32[]{:S(2)}, u32[]{:S(2)}) collective-permute-start(bf16[192,384]{1,0:T(8,128)(2,1)} %collective-permute-done.4.near_ref), channel_id=1, source_target_pairs={{0,4},{4,0},{8,12},{12,8},{16,20},{20,16},{24,28},{28,24},{1,5},{5... | collective-permute-start | bytes 442376 | tf_op jit(solution)/shard_map/ppermute | solution.py:390
  88.0 44.7 %collective-permute-start.10 = (bf16[384,768]{1,0:T(8,128)(2,1)}, bf16[384,768]{1,0:T(8,128)(2,1)}, u32[]{:S(2)}, u32[]{:S(2)}) collective-permute-start(bf16[384,768]{1,0:T(8,128)(2,1)} %collective-permute-done.9.near_ref.refs_9_), channel_id=1, source_target_pairs={{0,4},{4,0},{8,12},{12,8},{16,20},{20,16},{24,28},{28,24},{1,5},{5... | collective-permute-start | bytes 1769480 | tf_op jit(solution)/shard_map/ppermute | solution.py:390
  149.6 59.3 %collective-permute-start.17 = (bf16[384,768]{1,0:T(8,128)(2,1)}, bf16[384,768]{1,0:T(8,128)(2,1)}, u32[]{:S(2)}, u32[]{:S(2)}) collective-permute-start(bf16[384,768]{1,0:T(8,128)(2,1)} %dynamic-slice_bitcast_fusion.3), channel_id=1, source_target_pairs={{0,2},{1,3},{2,0},{3,1},{4,6},{5,7},{6,4},{7,5},{8,10},{9,11},{10,... | collective-permute-start | bytes 1769480 | tf_op jit(solution)/shard_map/ppermute | solution.py:389
  162.6 46.8 %collective-permute-start.19 = (bf16[384,768]{1,0:T(8,128)(2,1)}, bf16[384,768]{1,0:T(8,128)(2,1)}, u32[]{:S(2)}, u32[]{:S(2)}) collective-permute-start(bf16[384,768]{1,0:T(8,128)(2,1)} %dynamic-slice_bitcast_fusion.2), channel_id=1, source_target_pairs={{0,2},{1,3},{2,0},{3,1},{4,6},{5,7},{6,4},{7,5},{8,10},{9,11},{10,... | collective-permute-start | bytes 1769480 | tf_op jit(solution)/shard_map/ppermute | solution.py:389
  164.2 32.3 %collective-permute-start.15 = (bf16[192,384]{1,0:T(8,128)(2,1)}, bf16[192,384]{1,0:T(8,128)(2,1)}, u32[]{:S(2)}, u32[]{:S(2)}) collective-permute-start(bf16[192,384]{1,0:T(8,128)(2,1)} %collective-permute-done.14.near_ref), channel_id=1, source_target_pairs={{0,4},{4,0},{8,12},{12,8},{16,20},{20,16},{24,28},{28,24},{1,5},{5... | collective-permute-start | bytes 442376 | tf_op jit(solution)/shard_map/ppermute | solution.py:390
  209.4 43.7 %collective-permute-start.20 = (bf16[384,768]{1,0:T(8,128)(2,1)}, bf16[384,768]{1,0:T(8,128)(2,1)}, u32[]{:S(2)}, u32[]{:S(2)}) collective-permute-start(bf16[384,768]{1,0:T(8,128)(2,1)} %collective-permute-done.19.near_ref.refs_6_), channel_id=1, source_target_pairs={{0,4},{4,0},{8,12},{12,8},{16,20},{20,16},{24,28},{28,24},{1,5},{5... | collective-permute-start | bytes 1769480 | tf_op jit(solution)/shard_map/ppermute | solution.py:390
  299.7 37.4 %collective-permute-start.47 = (bf16[1,768,768]{2,1,0:T(8,128)(2,1)}, bf16[1,768,768]{2,1,0:T(8,128)(2,1)}, u32[]{:S(2)}, u32[]{:S(2)}) collective-permute-start(bf16[1,768,768]{2,1,0:T(8,128)(2,1)} %bitcast.87), channel_id=1, source_target_pairs={{0,2},{1,3},{2,0},{3,1},{4,6},{5,7},{6,4},{7,5},{8,10},{9,11},{10,... | collective-permute-start | bytes 3538952 | tf_op jit(solution)/shard_map/ppermute | solution.py:389
  310.7 30.5 %collective-permute-start.55 = (bf16[2,1,4,96,768]{4,3,2,1,0:T(8,128)(2,1)}, bf16[2,1,4,96,768]{4,3,2,1,0:T(8,128)(2,1)}, u32[]{:S(2)}, u32[]{:S(2)}) collective-permute-start(bf16[2,1,4,96,768]{4,3,2,1,0:T(8,128)(2,1)} %pad_maximum_fusion.1), channel_id=1, source_target_pairs={{0,4},{4,0},{8,12},{12,8},{16,20},{20,16},{24,28},{28,24},{1,5},{5... | collective-permute-start | bytes 3538952 | tf_op jit(solution)/shard_map/ppermute | solution.py:390
  324.0 42.4 %collective-permute-start.24 = (bf16[512,768]{1,0:T(8,128)(2,1)}, bf16[512,768]{1,0:T(8,128)(2,1)}, u32[]{:S(2)}, u32[]{:S(2)}) collective-permute-start(bf16[512,768]{1,0:T(8,128)(2,1)} %qkv_back.2.refs_0_), channel_id=1, source_target_pairs={{0,1},{1,0},{2,3},{3,2},{4,5},{5,4},{6,7},{7,6},{8,9},{9,8},{10,11... | collective-permute-start | bytes 2359304 | tf_op jit(solution)/shard_map/ppermute | solution.py:388
  328.9 27.9 %collective-permute-start.39 = (bf16[2,2,4,96,192]{4,3,2,1,0:T(8,128)(2,1)}, bf16[2,2,4,96,192]{4,3,2,1,0:T(8,128)(2,1)}, u32[]{:S(2)}, u32[]{:S(2)}) collective-permute-start(bf16[2,2,4,96,192]{4,3,2,1,0:T(8,128)(2,1)} %pad_maximum_fusion.4), channel_id=1, source_target_pairs={{0,4},{4,0},{8,12},{12,8},{16,20},{20,16},{24,28},{28,24},{1,5},{5... | collective-permute-start | bytes 1769480 | tf_op jit(solution)/shard_map/ppermute | solution.py:390
  332.3 28.6 %collective-permute-start.35 = (bf16[2,768,192]{1,2,0:T(8,128)(2,1)}, bf16[2,768,192]{1,2,0:T(8,128)(2,1)}, u32[]{:S(2)}, u32[]{:S(2)}) collective-permute-start(bf16[2,768,192]{1,2,0:T(8,128)(2,1)} %copy.152), channel_id=1, source_target_pairs={{0,2},{1,3},{2,0},{3,1},{4,6},{5,7},{6,4},{7,5},{8,10},{9,11},{10,... | collective-permute-start | bytes 1769480 | tf_op jit(solution)/shard_map/ppermute | solution.py:389
  340.4 57.0 %collective-permute-start.48 = (bf16[1,4,96,768]{3,2,1,0:T(8,128)(2,1)}, bf16[1,4,96,768]{3,2,1,0:T(8,128)(2,1)}, u32[]{:S(2)}, u32[]{:S(2)}) collective-permute-start(bf16[1,4,96,768]{3,2,1,0:T(8,128)(2,1)} %fusion.16), channel_id=1, source_target_pairs={{0,4},{4,0},{8,12},{12,8},{16,20},{20,16},{24,28},{28,24},{1,5},{5... | collective-permute-start | bytes 1769480 | tf_op jit(solution)/shard_map/ppermute | solution.py:390
  343.8 55.5 %collective-permute-start.56 = (bf16[1,4,96,768]{3,2,1,0:T(8,128)(2,1)}, bf16[1,4,96,768]{3,2,1,0:T(8,128)(2,1)}, u32[]{:S(2)}, u32[]{:S(2)}) collective-permute-start(bf16[1,4,96,768]{3,2,1,0:T(8,128)(2,1)} %fusion.1), channel_id=1, source_target_pairs={{0,2},{1,3},{2,0},{3,1},{4,6},{5,7},{6,4},{7,5},{8,10},{9,11},{10,... | collective-permute-start | bytes 1769480 | tf_op jit(solution)/shard_map/ppermute | solution.py:389
  359.4 33.3 %collective-permute-start.40 = (bf16[2,4,96,192]{3,2,1,0:T(8,128)(2,1)}, bf16[2,4,96,192]{3,2,1,0:T(8,128)(2,1)}, u32[]{:S(2)}, u32[]{:S(2)}) collective-permute-start(bf16[2,4,96,192]{3,2,1,0:T(8,128)(2,1)} %fusion.9), channel_id=1, source_target_pairs={{0,2},{1,3},{2,0},{3,1},{4,6},{5,7},{6,4},{7,5},{8,10},{9,11},{10,... | collective-permute-start | bytes 884744 | tf_op jit(solution)/shard_map/ppermute | solution.py:389
  365.9 28.8 %collective-permute-start.36 = (bf16[2,4,96,192]{3,2,1,0:T(8,128)(2,1)}, bf16[2,4,96,192]{3,2,1,0:T(8,128)(2,1)}, u32[]{:S(2)}, u32[]{:S(2)}) collective-permute-start(bf16[2,4,96,192]{3,2,1,0:T(8,128)(2,1)} %fusion.21), channel_id=1, source_target_pairs={{0,4},{4,0},{8,12},{12,8},{16,20},{20,16},{24,28},{28,24},{1,5},{5... | collective-permute-start | bytes 884744 | tf_op jit(solution)/shard_map/ppermute | solution.py:390
  378.8 61.7 %collective-permute-start.25 = (bf16[512,768]{1,0:T(8,128)(2,1)}, bf16[512,768]{1,0:T(8,128)(2,1)}, u32[]{:S(2)}, u32[]{:S(2)}) collective-permute-start(bf16[512,768]{1,0:T(8,128)(2,1)} %get-tuple-element.154.self_ref), channel_id=1, source_target_pairs={{0,1},{1,0},{2,3},{3,2},{4,5},{5,4},{6,7},{7,6},{8,9},{9,8},{10,11... | collective-permute-start | bytes 2359304 | tf_op jit(solution)/shard_map/ppermute | solution.py:388
  392.7 117.3 %collective-permute-start.43 = (bf16[1,768,768]{2,1,0:T(8,128)(2,1)}, bf16[1,768,768]{2,1,0:T(8,128)(2,1)}, u32[]{:S(2)}, u32[]{:S(2)}) collective-permute-start(bf16[1,768,768]{2,1,0:T(8,128)(2,1)} %bitcast.78), channel_id=1, source_target_pairs={{0,2},{1,3},{2,0},{3,1},{4,6},{5,7},{6,4},{7,5},{8,10},{9,11},{10,... | collective-permute-start | bytes 3538952 | tf_op jit(solution)/shard_map/ppermute | solution.py:389
  394.7 118.4 %collective-permute-start.51 = (bf16[2,1,4,96,768]{4,3,2,1,0:T(8,128)(2,1)}, bf16[2,1,4,96,768]{4,3,2,1,0:T(8,128)(2,1)}, u32[]{:S(2)}, u32[]{:S(2)}) collective-permute-start(bf16[2,1,4,96,768]{4,3,2,1,0:T(8,128)(2,1)} %pad_maximum_fusion), channel_id=1, source_target_pairs={{0,4},{4,0},{8,12},{12,8},{16,20},{20,16},{24,28},{28,24},{1,5},{5... | collective-permute-start | bytes 3538952 | tf_op jit(solution)/shard_map/ppermute | solution.py:390
  483.5 32.7 %collective-permute-start.26 = (bf16[256,768]{1,0:T(8,128)(2,1)}, bf16[256,768]{1,0:T(8,128)(2,1)}, u32[]{:S(2)}, u32[]{:S(2)}) collective-permute-start(bf16[256,768]{1,0:T(8,128)(2,1)} %slice.439), channel_id=1, source_target_pairs={{0,1},{1,0},{2,3},{3,2},{4,5},{5,4},{6,7},{7,6},{8,9},{9,8},{10,11... | collective-permute-start | bytes 1179656 | tf_op jit(solution)/shard_map/ppermute | solution.py:388
  512.4 30.5 %collective-permute-start.44 = (bf16[1,4,96,768]{3,2,1,0:T(8,128)(2,1)}, bf16[1,4,96,768]{3,2,1,0:T(8,128)(2,1)}, u32[]{:S(2)}, u32[]{:S(2)}) collective-permute-start(bf16[1,4,96,768]{3,2,1,0:T(8,128)(2,1)} %fusion.18), channel_id=1, source_target_pairs={{0,4},{4,0},{8,12},{12,8},{16,20},{20,16},{24,28},{28,24},{1,5},{5... | collective-permute-start | bytes 1769480 | tf_op jit(solution)/shard_map/ppermute | solution.py:390
  515.6 30.3 %collective-permute-start.52 = (bf16[1,4,96,768]{3,2,1,0:T(8,128)(2,1)}, bf16[1,4,96,768]{3,2,1,0:T(8,128)(2,1)S(1)}, u32[]{:S(2)}, u32[]{:S(2)}) collective-permute-start(bf16[1,4,96,768]{3,2,1,0:T(8,128)(2,1)} %fusion.5), channel_id=1, source_target_pairs={{0,2},{1,3},{2,0},{3,1},{4,6},{5,7},{6,4},{7,5},{8,10},{9,11},{10,... | collective-permute-start | bytes 1769480 | tf_op jit(solution)/shard_map/ppermute | solution.py:389
  (245 other events, 1476.2 us)

commit v2 on v0

v2 whole, which is shorter than its diff:
```python
from functools import partial

import jax
import jax.numpy as jnp
from jax import lax
from jax.experimental import pallas as pl
from jax.experimental.pallas import tpu as pltpu
from jax.sharding import PartitionSpec as P

HEAD_DIM = 64
LAYERS = 2
LONG_LEN = 512
SHORT_LEN = 128
LONG_DEV = 1
SHORT_DEV = 4

EPS = 1e-06
MASKED = -1e30
BOTH = ("dp", "tensor")
F32 = jnp.float32
BF16 = jnp.bfloat16
VMEM_LIMIT = 60 * 1024 * 1024

X, Y, CORE, DP, SHARD, LENGTHS = range(6)


def nt(left, right):
    return lax.dot_general(left, right, (((1,), (1,)), ((), ())), preferred_element_type=F32)


def nn(left, right):
    return jnp.dot(left, right, preferred_element_type=F32)


def tn(left, right):
    return lax.dot_general(left, right, (((0,), (0,)), ((), ())), preferred_element_type=F32)


def merge(values):
    return values.reshape(values.shape[0] * values.shape[1], values.shape[2])


def bound_of(top_ref):
    return jnp.max(top_ref[...]) * 0.25 + EPS


def halves(scal, width):
    part = width // 2
    near = scal[Y]
    first = pl.ds(pl.multiple_of(near * part, part), part)
    second = pl.ds(pl.multiple_of((1 - near) * part, part), part)
    return first, second


class Load:
    def __init__(self, shape, dtype, pieces):
        self.shape, self.dtype, self.pieces = tuple(shape), dtype, pieces


class Store:
    def __init__(self, shape, dtype, pieces=((),)):
        self.shape, self.dtype, self.pieces = tuple(shape), dtype, pieces


def view(ref, index):
    return ref.at[index] if index else ref


class Arriving:
    def __init__(self, ref, copies):
        self.ref, self.copies, self.waited = ref, copies, set()

    def wait(self, piece):
        if piece not in self.waited:
            self.copies[piece].wait()
            self.waited.add(piece)
        return self.ref

    def all(self):
        for piece in range(len(self.copies)):
            self.wait(piece)
        return self.ref


class Leaving:
    def __init__(self, ref, copies):
        self.ref, self.copies, self.started = ref, copies, set()

    def flush(self, piece=0):
        self.copies[piece].start()
        self.started.add(piece)


def stream(scal, body, loads, stores, name, flops=0, scratch=(), after=()):
    arrays = []

    def slot(array):
        for i, known in enumerate(arrays):
            if known is array:
                return i
        arrays.append(array)
        return len(arrays) - 1

    plan = [[(slot(a), src, dst) for a, src, dst in load.pieces] for load in loads]
    first_out = len(arrays) + len(after)
    n_in = sum(len(p) for p in plan)
    n_out = sum(len(st.pieces) for st in stores)

    def kernel(scal_ref, *refs):
        sources = refs[: len(arrays)]
        targets = refs[first_out : first_out + len(stores)]
        at = first_out + len(stores)
        vin, at = refs[at : at + len(loads)], at + len(loads)
        vout, at = refs[at : at + len(stores)], at + len(stores)
        extra, (sem_in, sem_out) = refs[at:-2], refs[-2:]
        count = 0
        arriving = []
        for pieces, ref in zip(plan, vin):
            copies = []
            for i, src, dst in pieces:
                copies.append(pltpu.make_async_copy(view(sources[i], src), view(ref, dst), sem_in.at[count]))
                count += 1
            arriving.append(Arriving(ref, copies))
        for piece in range(max(len(p) for p in plan)):
            for a in arriving:
                if piece < len(a.copies):
                    a.copies[piece].start()
        count = 0
        leaving = []
        for st, ref, target in zip(stores, vout, targets):
            copies = []
            for index in st.pieces:
                copies.append(pltpu.make_async_copy(view(ref, index), view(target, index), sem_out.at[count]))
                count += 1
            leaving.append(Leaving(ref, copies))
        body(scal_ref, arriving, leaving, *extra)
        for a in arriving:
            a.all()
        for out in leaving:
            for piece, copy in enumerate(out.copies):
                if piece not in out.started:
                    copy.start()
        for out in leaving:
            for copy in out.copies:
                copy.wait()

    moved = sum(a.size * a.dtype.itemsize for a in arrays)
    for st in stores:
        size = jnp.dtype(st.dtype).itemsize
        for n in st.shape:
            size *= n
        moved += size
    anywhere = pl.BlockSpec(memory_space=pl.ANY)
    return pl.pallas_call(
        kernel,
        in_specs=[pl.BlockSpec(memory_space=pltpu.SMEM)] + [anywhere] * first_out,
        out_specs=[anywhere] * len(stores),
        out_shape=[jax.ShapeDtypeStruct(st.shape, st.dtype) for st in stores],
        scratch_shapes=[pltpu.VMEM(x.shape, x.dtype) for x in list(loads) + list(stores)]
        + list(scratch)
        + [pltpu.SemaphoreType.DMA((n_in,)), pltpu.SemaphoreType.DMA((n_out,))],
        name=name,
        cost_estimate=pl.CostEstimate(flops=int(flops), bytes_accessed=int(moved), transcendentals=0),
        compiler_params=pltpu.CompilerParams(vmem_limit_bytes=VMEM_LIMIT),
    )(scal, *arrays, *after)


ALL = slice(None)


def span(i, size):
    return pl.ds(i * size, size)


def whole_in(a):
    return Load(a.shape, a.dtype, [(a, (), ())])


def layer_in(a, layer):
    return Load(a.shape[1:], a.dtype, [(a, (layer,), ())])


def rows_in(a, count, swap=False):
    size = a.shape[0] // count
    turn = count // 2 if swap else 0
    return Load(a.shape, a.dtype, [(a, (span((i + turn) % count, size),), (span(i, size),)) for i in range(count)])


def pair_in(mine, other, count):
    rows, width = mine.shape
    size = 2 * rows // count
    half = count // 2
    return Load(
        (2 * rows, width),
        mine.dtype,
        [((mine if i < half else other), (span(i % half, size),), (span(i, size),)) for i in range(count)],
    )


def sides_in(a, count):
    size = a.shape[1] // count
    return Load(a.shape, a.dtype, [(a, (ALL, span(i, size)), (ALL, span(i, size))) for i in range(count)])


def per_side_in(a):
    return Load(a.shape, a.dtype, [(a, (i,), (i,)) for i in range(a.shape[0])])


def rows_out(shape, dtype, count):
    size = shape[0] // count
    return Store(shape, dtype, [(span(i, size),) for i in range(count)])


def sides_out(shape, dtype, count):
    size = shape[1] // count
    return Store(shape, dtype, [(ALL, span(i, size)) for i in range(count)])


def side_rows_out(shape, dtype, lead, count):
    size = shape[1 + lead] // count
    return Store(shape, dtype, [(s,) + (ALL,) * lead + (span(i, size),) for s in range(2) for i in range(count)])


def per_side_out(shape, dtype):
    return Store(shape, dtype, [(i,) for i in range(shape[0])])


B_OUT, GAIN_ONE, SHIFT_ONE, B_DOWN, GAIN_TWO, SHIFT_TWO, B_Q, B_V, B_UP, VECS = range(10)


def vec(ref, layer, row, width=None):
    at = layer * VECS + row
    return ref[at : at + 1, :] if width is None else ref[at : at + 1, 0:width]


def start_kernel(scal, hidden_ref, bout_ref, gain_ref, shift_ref, bdown_ref, bqv_ref, bup_ref, vecs_ref, small_ref, top_ref, sums_ref):
    heads_width = bqv_ref.shape[2]
    vecs_ref[...] = jnp.zeros(vecs_ref.shape, F32)
    small_ref[...] = jnp.zeros(small_ref.shape, F32)
    for layer in range(LAYERS):
        base = layer * VECS
        one = slice(layer, layer + 1)
        vecs_ref[base + B_OUT : base + B_OUT + 1, :] = bout_ref[one, :]
        vecs_ref[base + B_DOWN : base + B_DOWN + 1, :] = bdown_ref[one, :]
        vecs_ref[base + GAIN_ONE : base + GAIN_ONE + 1, :] = gain_ref[layer, 0:1, :]
        vecs_ref[base + GAIN_TWO : base + GAIN_TWO + 1, :] = gain_ref[layer, 1:2, :]
        vecs_ref[base + SHIFT_ONE : base + SHIFT_ONE + 1, :] = shift_ref[layer, 0:1, :]
        vecs_ref[base + SHIFT_TWO : base + SHIFT_TWO + 1, :] = shift_ref[layer, 1:2, :]
        for ref, at in ((vecs_ref, base + B_Q), (small_ref, 3 * layer)):
            ref[at : at + 1, 0:heads_width] = bqv_ref[layer, 0:1, :]
            ref[at + 1 : at + 2, 0:heads_width] = bqv_ref[layer, 1:2, :]
            ref[at + 2 : at + 3, :] = bup_ref[one, :]
    values = hidden_ref[...].astype(F32)
    top_ref[...] = jnp.full(top_ref.shape, jnp.max(jnp.abs(values)), F32)
    sums_ref[...] = jnp.full((1, 128), jnp.sum(values * values), F32)


def halves_kernel(scal, wqkv_ref, wout_ref, wup_ref, wdown_ref, *refs):
    att_ref, up_ref, down_ref = refs[-3:]
    att_ref[0:3] = wqkv_ref[...]
    att_ref[3] = wout_ref[...]
    up_ref[...] = wup_ref[...]
    down_ref[...] = wdown_ref[...]


def row_ids(scal, slots, half_rows):
    rows = 2 * half_rows
    slot = slots + half_rows * scal[CORE]
    slot = jnp.where(slot >= rows, slot - rows, slot) + scal[X] * rows
    short = slot - LONG_DEV * LONG_LEN
    is_long = short < 0
    row = jnp.where(is_long, slot // LONG_LEN, LONG_DEV + short // SHORT_LEN)
    place = jnp.where(is_long, slot % LONG_LEN, short % SHORT_LEN)
    length = jnp.zeros_like(row)
    for i in range(LONG_DEV + SHORT_DEV):
        length = jnp.where(row == i, scal[LENGTHS + i], length)
    return row, place < length


HEADS = ((0, 128, 0), (0, 128, 1), (128, 192, None))


def lane_mask(rows, which):
    lane = lax.broadcasted_iota(jnp.int32, (rows, 128), 1)
    return (lane < HEAD_DIM) if which == 0 else (lane >= HEAD_DIM)


def only_head(values, which):
    if which is None:
        return values
    return jnp.where(lane_mask(values.shape[0], which), values, jnp.zeros_like(values))


def largest(values):
    return jnp.max(jnp.abs(values))


def put_top(out, tops):
    top = tops[0]
    for other in tops[1:]:
        top = jnp.maximum(top, other)
    out.ref[...] = jnp.full(out.ref.shape, top, F32)
    out.flush()


def attend_body(layer, count, scal, ins, outs, bias_ref):
    x_in, top_in, vecs_in, own_in, near_in, far_in, small_in = ins
    low_out, fac_out, qkv_out, ctx_out, e_out, rinv_out, top_out = outs
    low_ref, qkv_ref, ctx_ref, e_ref, rinv_ref = (o.ref for o in (low_out, qkv_out, ctx_out, e_out, rinv_out))
    rows, width = low_ref.shape
    heads_width = qkv_ref.shape[3]
    first, second = halves(scal, width)
    q_row, _ = row_ids(scal, lax.broadcasted_iota(jnp.int32, (rows, 1), 0), rows // 2)
    k_row, k_live = row_ids(scal, lax.broadcasted_iota(jnp.int32, (1, rows), 1), rows // 2)
    k_row = jnp.where(k_live, k_row, -1)
    bias_ref[...] = jnp.where(q_row == k_row, 0.0, MASKED)
    bound = bound_of(top_in.all())
    size = rows // count
    vecs_ref = vecs_in.all()
    for i in range(count):
        place = slice(i * size, (i + 1) * size)
        tangent = jnp.tanh(x_in.wait(i)[place, :].astype(F32) * (1.0 / bound))
        low = (bound * tangent).astype(BF16)
        low_ref[place, :] = low
        low_out.flush(i)
        fac_out.ref[place, :] = (1.0 - tangent * tangent).astype(BF16)
        fac_out.flush(i)
        own_ref = own_in.all()
        for j in range(3):
            values = nt(low, own_ref[j])
            if j != 1:
                values = values + vec(vecs_ref, layer, B_Q + j // 2, heads_width)
            qkv_ref[0, j, place, :] = values.astype(BF16)
    qkv_out.flush(0)
    scale = HEAD_DIM ** (-0.5)
    chunk = 128
    chunks = rows // chunk
    tops = []
    for side in range(2):
        if side == 1:
            near_ref, far_ref, small_ref = near_in.all(), far_in.all(), small_in.all()
            for j in range(3):
                values = nt(low_ref[:, first], near_ref[j]) + nt(low_ref[:, second], far_ref[j])
                if j != 1:
                    at = 3 * layer + j // 2
                    values = values + small_ref[at : at + 1, 0:heads_width]
                qkv_ref[1, j] = values.astype(BF16)
            qkv_out.flush(1)
        heads = []
        for h, (lo, hi, which) in enumerate(HEADS):
            keys = only_head(qkv_ref[side, 1, :, lo:hi], which)
            heads.append((h, lo, hi, which, keys, qkv_ref[side, 2, :, lo:hi]))
        left = lane_mask(chunk, 0)
        for i in range(chunks):
            place = slice(i * chunk, (i + 1) * chunk)
            done = []
            for h, lo, hi, which, keys, vals in heads:
                scores = nt(qkv_ref[side, 0, place, lo:hi], keys) * scale + bias_ref[place, :]
                weights = jnp.exp(scores - jnp.max(scores, axis=1, keepdims=True))
                inverse = 1.0 / jnp.sum(weights, axis=1, keepdims=True)
                low = weights.astype(BF16)
                e_ref[side, h, place, :] = low
                done.append((nn(low, vals) * inverse, inverse))
            pair = jnp.where(left, done[0][0], done[1][0])
            ctx_ref[side, place, 0:128] = pair
            ctx_ref[side, place, 128:192] = done[2][0]
            tops += [largest(pair), largest(done[2][0])]
            rinv_ref[side, place, 0:128] = jnp.where(left, done[0][1], done[1][1])
            rinv_ref[side, place, 128:192] = jnp.broadcast_to(done[2][1], (chunk, HEAD_DIM))
            for out in (e_out, ctx_out, rinv_out):
                out.flush(side * chunks + i)
    put_top(top_out, tops)


def out_body(count, scal, ins, outs):
    top_in, ctx_in, own_in, near_in, far_in = ins
    c_out, fac_out, o_out = outs
    bound = bound_of(top_in.all())
    rows, width = o_out.ref.shape
    size = rows // count
    for i in range(count):
        place = slice(i * size, (i + 1) * size)
        tangent = jnp.tanh(ctx_in.wait(i)[:, place, :] * (1.0 / bound))
        low = (bound * tangent).astype(BF16)
        c_out.ref[:, place, :] = low
        c_out.flush(i)
        fac_out.ref[:, place, :] = (1.0 - tangent * tangent).astype(BF16)
        fac_out.flush(i)
        own_ref = own_in.all()
        for part, load in zip(halves(scal, width), (near_in, far_in)):
            o_out.ref[place, part] = (nn(low[0], own_ref[:, part]) + nn(low[1], load.all()[3])).astype(BF16)
        o_out.flush(i)


def norm_forward(mixed, gain, shift):
    centred = mixed - jnp.mean(mixed, axis=1, keepdims=True)
    inverse = lax.rsqrt(jnp.mean(centred * centred, axis=1, keepdims=True) + EPS)
    unit = centred * inverse
    return unit * gain + shift, unit, inverse


def lane_fill(value):
    return jnp.full((1, 128), value, F32)


def norm_body(layer, second, count, scal, ins, outs):
    vecs_in, x_in, self_in, recv_in = ins
    h_out, unit_out, inv_out, sums_out, top_out = outs
    rows, width = h_out.ref.shape
    size = rows // count
    vecs_ref = vecs_in.all()
    bias = vec(vecs_ref, layer, B_DOWN if second else B_OUT)
    gain = vec(vecs_ref, layer, GAIN_TWO if second else GAIN_ONE)
    shift = vec(vecs_ref, layer, SHIFT_TWO if second else SHIFT_ONE)
    tops, branch_sum, result_sum = [], 0.0, 0.0
    for i in range(count):
        place = slice(i * size, (i + 1) * size)
        branch = self_in.wait(i)[place, :].astype(F32) + recv_in.wait(i)[place, :].astype(F32) + bias
        result, unit, inverse = norm_forward(x_in.wait(i)[place, :].astype(F32) + branch, gain, shift)
        h_out.ref[place, :] = result
        h_out.flush(i)
        unit_out.ref[place, :] = unit.astype(unit_out.ref.dtype)
        unit_out.flush(i)
        inv_out.ref[place, :] = jnp.broadcast_to(inverse, (size, 128))
        inv_out.flush(i)
        tops.append(largest(result))
        if i < count // 2:
            branch_sum = branch_sum + jnp.sum(branch * branch)
            result_sum = result_sum + jnp.sum(result * result)
    sums_out.ref[0:1, :] = lane_fill(branch_sum)
    sums_out.ref[1:2, :] = lane_fill(result_sum)
    sums_out.flush()
    put_top(top_out, tops)


def up_body(layer, count, scal, ins, outs):
    top_in, h_in, vecs_in, own_in, near_in, far_in, small_in = ins
    low_out, fac_out, g_out, slope_out, top_out = outs
    low_ref = low_out.ref
    rows, width = low_ref.shape
    size = rows // count
    bound = bound_of(top_in.all())
    first, second = halves(scal, width)
    tops = []
    for i in range(count):
        place = slice(i * size, (i + 1) * size)
        tangent = jnp.tanh(h_in.wait(i)[place, :] * (1.0 / bound))
        low = (bound * tangent).astype(BF16)
        low_ref[place, :] = low
        low_out.flush(i)
        fac_out.ref[place, :] = (1.0 - tangent * tangent).astype(BF16)
        fac_out.flush(i)
        for side in range(2):
            if side == 0:
                units = nn(low, own_in.all()[...]) + vec(vecs_in.all(), layer, B_UP)
            else:
                units = nn(low_ref[place, first], near_in.all()[...]) + nn(low_ref[place, second], far_in.all()[...])
                units = units + small_in.all()[3 * layer + 2 : 3 * layer + 3, :]
            area = 0.5 + 0.5 * lax.erf(units * (0.5**0.5))
            density = jnp.exp(-0.5 * units * units) * 0.3989422804014327
            active = units * area
            g_out.ref[side, place, :] = active
            slope_out.ref[side, place, :] = (area + units * density).astype(BF16)
            tops.append(largest(active))
        g_out.flush(i)
        slope_out.flush(i)
    put_top(top_out, tops)


def down_body(count, scal, ins, outs):
    top_in, g_in, slope_in, own_in, near_in, far_in = ins
    low_out, fac_out, f_out = outs
    low_ref = low_out.ref
    rows, width = f_out.ref.shape
    size = rows // count
    bound = bound_of(top_in.all())
    first, second = halves(scal, low_ref.shape[2])
    for i in range(count):
        place = slice(i * size, (i + 1) * size)
        tangent = jnp.tanh(g_in.wait(i)[:, place, :] * (1.0 / bound))
        low_ref[:, place, :] = (bound * tangent).astype(BF16)
        low_out.flush(i)
        slope = slope_in.wait(i)[:, place, :].astype(F32)
        fac_out.ref[:, place, :] = ((1.0 - tangent * tangent) * slope).astype(BF16)
        fac_out.flush(i)
        f_out.ref[place, :] = (
            nn(low_ref[0, place, :], own_in.all()[...])
            + nn(low_ref[1, place, first], near_in.all()[...])
            + nn(low_ref[1, place, second], far_in.all()[...])
        ).astype(BF16)
        f_out.flush(i)


def norm_back(grad, unit, inverse, gain):
    scaled = grad * gain
    return (
        scaled
        - jnp.mean(scaled, axis=1, keepdims=True)
        - unit * jnp.mean(scaled * unit, axis=1, keepdims=True)
    ) * inverse


def column_sums(values):
    return jnp.sum(values, axis=0, keepdims=True)


def ffn_back_body(layer, last_layer, count, scal, ins, outs):
    vecs_in, ins = ins[0], ins[1:]
    if last_layer:
        (h_in, self_in, recv_in, cot_in), ins = ins[:4], ins[4:]
        result_out, fsum_out = outs[-2:]
    else:
        (self_in, recv_in, infac_in, skip_in, unit_in, inv_in), ins = ins[:6], ins[6:]
    fac_in, down_in, dnear_in, dfar_in, up_in, unear_in, ufar_in = ins
    dz_out, df_out, du_out, dh_out, sums_out, usum_out = outs[:6]
    rows, width = dz_out.ref.shape
    size = rows // count
    vecs_ref = vecs_in.all()
    gain = vec(vecs_ref, layer, GAIN_TWO)
    first, second = halves(scal, width)
    du_ref = du_out.ref
    totals = None
    unit_totals = None
    branch_sum = 0.0
    for i in range(count):
        place = slice(i * size, (i + 1) * size)
        mine = i < count // 2
        both = self_in.wait(i)[place, :].astype(F32) + recv_in.wait(i)[place, :].astype(F32)
        if last_layer:
            branch = both + vec(vecs_ref, layer, B_DOWN)
            result, unit, inverse = norm_forward(h_in.wait(i)[place, :] + branch, gain, vec(vecs_ref, layer, SHIFT_TWO))
            grad = cot_in.wait(i)[place, :].astype(F32)
            if mine:
                result_out.ref[place, :] = result.astype(BF16)
                result_out.flush(i)
                branch_sum = branch_sum + jnp.sum(branch * branch)
        else:
            grad = both * infac_in.wait(i)[place, :].astype(F32) + skip_in.wait(i)[place, :]
            unit = unit_in.wait(i)[place, :].astype(F32)
            inverse = inv_in.wait(i)[place, 0:1]
        mixed = norm_back(grad, unit, inverse, gain)
        low = mixed.astype(BF16)
        dz_out.ref[place, :] = mixed
        dz_out.flush(i)
        df_out.ref[place, :] = low
        df_out.flush(i)
        if mine:
            new = [column_sums(v) for v in (grad * unit, grad, low.astype(F32))]
            totals = new if totals is None else [a + b for a, b in zip(totals, new)]
        fac_ref = fac_in.wait(i)
        du_ref[0, place, :] = (nt(low, down_in.all()[...]) * fac_ref[0, place, :].astype(F32)).astype(BF16)
        for part, load in ((first, dnear_in), (second, dfar_in)):
            du_ref[1, place, part] = (nt(low, load.all()[...]) * fac_ref[1, place, part].astype(F32)).astype(BF16)
        du_out.flush(i)
        for part, load in ((first, unear_in), (second, ufar_in)):
            dh_out.ref[place, part] = (
                nt(du_ref[0, place, :], up_in.all()[part, :]) + nt(du_ref[1, place, :], load.all()[...])
            ).astype(BF16)
        dh_out.flush(i)
        new = [column_sums(du_ref[side, place, :].astype(F32)) for side in range(2)]
        unit_totals = new if unit_totals is None else [a + b for a, b in zip(unit_totals, new)]
    for row, values in enumerate(totals):
        sums_out.ref[row : row + 1, :] = values
    for row, values in enumerate(unit_totals):
        usum_out.ref[row : row + 1, :] = values
    if last_layer:
        fsum_out.ref[...] = lane_fill(branch_sum)


def attn_back_body(layer, split, count, scal, ins, outs, da_scratch):
    (vecs_in, self_in, recv_in, hfac_in, skip_in, unit_in, inv_in, wout_in, cfac_in, rinv_in, ctx_in, qkv_in, e_in, wqkv_in,
     near_in, far_in) = ins
    dz_out, do_out, d_out, sums_out, hsum_out, da_out = outs[:6]
    rows, width = dz_out.ref.shape
    heads_width = qkv_in.ref.shape[3]
    size = rows // count
    first, second = halves(scal, width)
    gain = vec(vecs_in.all(), layer, GAIN_ONE)
    totals = None
    for i in range(count):
        place = slice(i * size, (i + 1) * size)
        grad = self_in.wait(i)[place, :].astype(F32) + recv_in.wait(i)[place, :].astype(F32)
        grad = grad * hfac_in.wait(i)[place, :].astype(F32) + skip_in.wait(i)[place, :]
        unit = unit_in.wait(i)[place, :].astype(F32)
        mixed = norm_back(grad, unit, inv_in.wait(i)[place, 0:1], gain)
        low = mixed.astype(BF16)
        dz_out.ref[place, :] = mixed
        dz_out.flush(i)
        do_out.ref[place, :] = low
        do_out.flush(i)
        if i < count // 2:
            new = [column_sums(v) for v in (grad * unit, grad, low.astype(F32))]
            totals = new if totals is None else [a + b for a, b in zip(totals, new)]
    for row, values in enumerate(totals):
        sums_out.ref[row : row + 1, :] = values
    do_ref, d_ref = do_out.ref, d_out.ref
    scale = HEAD_DIM ** (-0.5)
    left = lane_mask(rows, 0)
    for side in range(2):
        if side == 0:
            grad_ctx = nt(do_ref[...], wout_in.all()[...])
        else:
            grad_ctx = nt(do_ref[:, first], near_in.all()[3]) + nt(do_ref[:, second], far_in.all()[3])
        grad_ctx = grad_ctx * cfac_in.wait(side)[side].astype(F32)
        low = (grad_ctx * rinv_in.wait(side)[side]).astype(BF16)
        product = low.astype(F32) * ctx_in.wait(side)[side]
        qkv_ref, e_ref = qkv_in.wait(side), e_in.wait(side)
        results = []
        for h, (lo, hi, which) in enumerate(HEADS):
            inner = jnp.sum(only_head(product[:, lo:hi], which), axis=1, keepdims=True)
            values = only_head(qkv_ref[side, 2, :, lo:hi], which)
            weights = e_ref[side, h]
            grad_weights = nt(low[:, lo:hi], values)
            grad_scores = (weights.astype(F32) * (grad_weights - inner)).astype(BF16)
            dq = nn(grad_scores, qkv_ref[side, 1, :, lo:hi]) * scale
            dk = tn(grad_scores, qkv_ref[side, 0, :, lo:hi]) * scale
            dv = tn(weights, low[:, lo:hi])
            results.append((dq, dk, dv))
        for j in range(3):
            pair = jnp.where(left, results[0][j], results[1][j]).astype(BF16)
            last = results[2][j].astype(BF16)
            d_ref[side, :, j * heads_width : j * heads_width + 128] = pair
            d_ref[side, :, j * heads_width + 128 : (j + 1) * heads_width] = last
            if j != 1:
                at = slice(j // 2, j // 2 + 1)
                hsum_out.ref[side, at, 0:128] = column_sums(pair.astype(F32))
                hsum_out.ref[side, at, 128:192] = column_sums(last.astype(F32))
        d_out.flush(side)
        if side == 0:
            da_scratch[...] = nn(d_ref[0], merge(wqkv_in.all()[...]))
    for i in range(2):
        place = slice(i * rows // 2, (i + 1) * rows // 2)
        for part, load in ((first, near_in), (second, far_in)):
            total = (da_scratch[place, part] + nn(d_ref[1, place, :], merge(load.ref[0:3]))).astype(BF16)
            if split:
                outs[5 + i].ref[:, part] = total
            else:
                da_out.ref[place, part] = total
        if split:
            outs[5 + i].flush()
        else:
            da_out.flush(i)


def bands(bit_value, count, band):
    return [pl.ds(pl.multiple_of((2 * k + bit_value) * band, band), band) for k in range(count)]


def grad_body(with_ffn, with_attn, band, scal, ins, outs, scratch):
    if with_ffn:
        (df_in, gq_in, hq_in, du_in), ins = ins[:4], ins[4:]
    if with_attn:
        a_in, d_in, do_in, c_in = ins

    def y_first(side):
        at = 0
        if with_ffn:
            at = gq_in.ref.shape[2]
            scratch[:, 0:at] = tn(df_in.all()[...], gq_in.all()[side])
        if with_attn:
            width = c_in.ref.shape[2]
            scratch[:, at : at + width] = tn(a_in.all()[...], d_in.all()[side, :, 2 * width : 3 * width])
            scratch[:, at + width : at + 2 * width] = tn(do_in.all()[...], c_in.all()[side])

    def x_first(side, put):
        at = 0
        if with_ffn:
            at = hq_in.ref.shape[1]
            put(slice(0, at), tn(hq_in.all()[...], du_in.all()[side]).astype(BF16))
        if with_attn:
            width = c_in.ref.shape[2]
            put(slice(at, at + 2 * width), tn(a_in.all()[...], d_in.all()[side, :, 0 : 2 * width]).astype(BF16))

    if len(outs) == 2:
        for side, out in ((0, outs[0]), (1, outs[1])):

            def put(columns, values, out=out):
                out.ref[0, :, columns] = values

            x_first(side, put)
            y_first(side)
            out.ref[1] = scratch[...].astype(BF16)
        return
    own_out, oth_out, keep_out, send_out = outs
    count = keep_out.ref.shape[1] // band
    mine, away = bands(scal[Y], count, band), bands(1 - scal[Y], count, band)
    for side, out in ((1, oth_out), (0, own_out)):

        def put(columns, values, out=out):
            out.ref[:, columns] = values

        x_first(side, put)
        out.flush()
        y_first(side)
        for k in range(count):
            place = slice(k * band, (k + 1) * band)
            send_out.ref[side, place, :] = scratch[away[k], :].astype(BF16)
            keep_out.ref[side, place, :] = scratch[mine[k], :].astype(BF16)
        send_out.flush(side)
        keep_out.flush(side)


def second_kernel(band, scal, own_ref, recv_ref, keep_ref, got_ref, xkeep_ref, xsend_ref, yown_ref, yoth_ref, scratch):
    count = xkeep_ref.shape[0] // band
    scratch[...] = own_ref[...].astype(F32) + recv_ref[...].astype(F32)
    mine, away = bands(scal[Y], count, band), bands(1 - scal[Y], count, band)
    yoth_ref[...] = (keep_ref[1].astype(F32) + got_ref[1].astype(F32)).astype(BF16)
    yown_ref[...] = (keep_ref[0].astype(F32) + got_ref[0].astype(F32)).astype(BF16)
    for k in range(count):
        place = slice(k * band, (k + 1) * band)
        xsend_ref[place, :] = scratch[away[k], :].astype(BF16)
        xkeep_ref[place, :] = scratch[mine[k], :].astype(BF16)


def fold_kernel(band, bit, scal, *refs):
    keep_out, send_out, scratch = refs[-3:]
    count = keep_out.shape[1] // band
    if len(refs) == 7:
        scratch[0] = refs[0][...].astype(F32) + refs[1][...].astype(F32)
        scratch[1] = refs[2][...].astype(F32) + refs[3][...].astype(F32)
    else:
        scratch[...] = refs[0][...].astype(F32) + refs[1][...].astype(F32)
    mine = (scal[DP] // bit) % 2
    for k, (take, give) in enumerate(zip(bands(mine, count, band), bands(1 - mine, count, band))):
        place = slice(k * band, (k + 1) * band)
        keep_out[:, place, :] = scratch[:, take, :].astype(BF16)
        send_out[:, place, :] = scratch[:, give, :].astype(BF16)


def final_kernel(heads_width, scal, a_keep, a_recv, b_keep, b_recv, c_keep, c_recv, qkv_ref, out_ref, up_ref, down_ref):
    width = up_ref.shape[2]
    first = a_keep[...].astype(F32) + a_recv[...].astype(F32)
    up_ref[1] = first[0]
    down_ref[1] = first[1]
    second = b_keep[...].astype(F32) + b_recv[...].astype(F32)
    up_ref[0] = second[0, :, 0:width]
    down_ref[0] = second[1, :, 0:width]
    third = c_keep[...].astype(F32) + c_recv[...].astype(F32)
    for layer, part in ((1, second[:, :, width:]), (0, third)):
        qkv_ref[layer, 0] = part[0, :, 0:heads_width]
        qkv_ref[layer, 1] = part[0, :, heads_width : 2 * heads_width]
        qkv_ref[layer, 2] = part[1, :, 0:heads_width]
        out_ref[layer] = part[1, :, heads_width : 2 * heads_width]


def pack_kernel(tensor_size, heads_width, scal, *refs):
    refs, out_ref = refs[:-1], refs[-1]
    out_ref[...] = jnp.zeros(out_ref.shape, F32)
    shard = scal[SHARD]
    for layer in range(LAYERS):
        one_ref, two_ref, heads_ref, units_ref = refs[4 * layer : 4 * layer + 4]
        base = layer * (6 + 2 * tensor_size)
        for row in range(3):
            out_ref[base + row] = one_ref[row : row + 1, :]
            out_ref[base + 3 + row] = two_ref[row : row + 1, :]
        for side in range(2):
            place = shard if side == 0 else shard + 2 - 4 * ((shard // 2) % 2)
            out_ref[base + 6 + place, :, 0:heads_width] = heads_ref[side, 0:1, :]
            out_ref[base + 6 + place, :, 256 : 256 + heads_width] = heads_ref[side, 1:2, :]
            out_ref[base + 6 + tensor_size + place] = units_ref[side : side + 1, :]
    base = LAYERS * (6 + 2 * tensor_size)
    for i, ref in enumerate(refs[4 * LAYERS :]):
        out_ref[base, :, 128 * i : 128 * (i + 1)] = ref[0:1, :]


def total_kernel(scal, in_ref, out_ref):
    devices = out_ref.shape[0]
    total = jnp.sum(in_ref[...].reshape(devices, -1, in_ref.shape[2]), axis=0, keepdims=True)
    out_ref[...] = jnp.broadcast_to(total, out_ref.shape)


def unpack_kernel(tensor_size, heads_width, count, scal, in_ref, hb_ref, ob_ref, gain_ref, shift_ref, ub_ref, db_ref, rms_ref):
    shard = scal[SHARD]
    for layer in range(LAYERS):
        base = layer * (6 + 2 * tensor_size)
        for k in range(2):
            gain_ref[layer, k : k + 1, :] = in_ref[base + 3 * k]
            shift_ref[layer, k : k + 1, :] = in_ref[base + 3 * k + 1]
        ob_ref[layer : layer + 1, :] = in_ref[base + 2]
        db_ref[layer : layer + 1, :] = in_ref[base + 5]
        heads = in_ref[base + 6 + shard]
        hb_ref[layer, 0:1, :] = heads[:, 0:heads_width]
        hb_ref[layer, 1:2, :] = heads[:, 256 : 256 + heads_width]
        ub_ref[layer : layer + 1, :] = in_ref[base + 6 + tensor_size + shard]
    base = LAYERS * (6 + 2 * tensor_size)
    row = jnp.sqrt(in_ref[base] * (1.0 / count))
    for layer in range(LAYERS):
        for k in range(3):
            i = 3 * layer + k
            rms_ref[layer : layer + 1, k : k + 1] = row[:, 128 * i : 128 * i + 1]


def dx_kernel(scal, self_ref, recv_ref, fac_ref, skip_ref, out_ref):
    grad = self_ref[...].astype(F32) + recv_ref[...].astype(F32)
    out_ref[...] = grad * fac_ref[...].astype(F32) + skip_ref[...]


def body(
    hidden,
    long_lengths,
    short_lengths,
    w_qkv,
    bias_qv,
    w_out,
    bias_out,
    ln_gain,
    ln_bias,
    w_up,
    bias_up,
    w_down,
    bias_down,
    cotangent,
):
    own_rows, width = hidden.shape
    rows = 2 * own_rows
    heads_width = w_qkv.shape[-1]
    units = w_up.shape[-1]
    dp_size, tensor_size = lax.axis_size("dp"), lax.axis_size("tensor")
    devices = dp_size * tensor_size
    count_model = float(own_rows * devices * width)
    dp_index, tensor_index = lax.axis_index("dp"), lax.axis_index("tensor")
    core_pairs = [(i, i ^ 1) for i in range(tensor_size)]
    x_pairs = [(i, i ^ 2) for i in range(tensor_size)]
    core_swap = lambda v: lax.ppermute(v, "tensor", core_pairs)
    x_swap = lambda v: lax.ppermute(v, "tensor", x_pairs)
    dp_swap = lambda v, bit: lax.ppermute(v, "dp", [(i, i ^ bit) for i in range(dp_size)])
    over_ranks = lambda top: lax.all_to_all(top, BOTH, 0, 0)

    scal = jnp.concatenate(
        [
            jnp.stack([tensor_index // 2, dp_index % 2, tensor_index % 2, dp_index, tensor_index]).astype(jnp.int32),
            long_lengths,
            short_lengths,
        ]
    )
    w_qkv = jnp.swapaxes(w_qkv, 2, 3)

    def run(kernel, ins, outs, name, flops=0, scratch=(), after=()):
        arrays = [array for array, _ in ins] + list(after)
        moved = sum(a.size * a.dtype.itemsize for a, _ in ins) + sum(
            jax.ShapeDtypeStruct(s, d).size * jnp.dtype(d).itemsize for s, d in outs
        )

        def trimmed(scal_ref, *refs):
            kernel(scal_ref, *refs[: len(ins)], *refs[len(arrays) :])

        return pl.pallas_call(
            trimmed,
            grid_spec=pltpu.PrefetchScalarGridSpec(
                num_scalar_prefetch=1,
                grid=(1,),
                in_specs=[s for _, s in ins] + [pl.BlockSpec(memory_space=pl.ANY)] * len(after),
                out_specs=[pl.BlockSpec(s, lambda i, t, n=len(s): (0,) * n) for s, _ in outs],
                scratch_shapes=list(scratch),
            ),
            out_shape=[jax.ShapeDtypeStruct(s, d) for s, d in outs],
            name=name,
            cost_estimate=pl.CostEstimate(flops=int(flops), bytes_accessed=int(moved), transcendentals=0),
            compiler_params=pltpu.CompilerParams(vmem_limit_bytes=VMEM_LIMIT),
        )(scal, *arrays)

    flow = partial(stream, scal)
    spec = pl.BlockSpec
    full = lambda a: (a, spec(a.shape, lambda i, s: (0,) * len(a.shape)))
    top_rows = lambda a, n: (a, spec((n,) + a.shape[1:], lambda i, s: (0,) * len(a.shape)))
    top_shape = (devices, 1, 128)
    top_store = Store(top_shape, F32)

    vecs, small, top, input_sum = run(
        start_kernel,
        [full(a) for a in (hidden, bias_out, ln_gain, ln_bias, bias_down, bias_qv, bias_up)],
        [((LAYERS * VECS, width), F32), ((LAYERS * 3, units), F32), (top_shape, F32), ((1, 128), F32)],
        "start",
    )
    top = over_ranks(top)
    other_hidden = core_swap(hidden)

    def weight_halves(l, after):
        sends = run(
            halves_kernel,
            [
                (w_qkv, spec((None, 3, heads_width, width // 2), lambda i, s: (l, 0, 0, s[Y]))),
                (w_out, spec((None, heads_width, width // 2), lambda i, s: (l, 0, s[Y]))),
                (w_up, spec((None, width // 2, units), lambda i, s: (l, s[Y], 0))),
                (w_down, spec((None, units // 2, width), lambda i, s: (l, s[Y], 0))),
            ],
            [((4, heads_width, width // 2), BF16), ((width // 2, units), BF16), ((units // 2, width), BF16)],
            "halves",
            after=after,
        )
        near = [x_swap(v) for v in sends]
        return list(zip(near, [dp_swap(v, 1) for v in near]))

    weights = [weight_halves(0, (input_sum,))]
    small = x_swap(small)

    saved = []
    square_terms = []
    states = None
    for l in range(LAYERS):
        last = l == LAYERS - 1
        first = l == 0
        (att_near, att_far), (up_near, up_far), (down_near, down_far) = weights[l]
        low_in, fac_in, qkv, ctx, soft, rinv, top = flow(
            partial(attend_body, l, 2),
            [pair_in(hidden, other_hidden, 2) if first else rows_in(states, 2), whole_in(top), whole_in(vecs), layer_in(w_qkv, l),
             whole_in(att_near), whole_in(att_far), whole_in(small)],
            [rows_out((rows, width), BF16, 2), rows_out((rows, width), BF16, 2), per_side_out((2, 3, rows, heads_width), BF16),
             side_rows_out((2, rows, heads_width), F32, 0, 4), side_rows_out((2, 3, rows, rows), BF16, 1, 4),
             side_rows_out((2, rows, heads_width), F32, 0, 4), top_store],
            "attend",
            flops=12 * rows * rows * 128 * 8,
            scratch=[pltpu.VMEM((rows, rows), F32)],
        )
        if first:
            weights.append(weight_halves(1, (top,)))
        top = over_ranks(top)
        low_ctx, fac_ctx, part = flow(
            partial(out_body, 2),
            [whole_in(top), sides_in(ctx, 2), layer_in(w_out, l), whole_in(att_near), whole_in(att_far)],
            [sides_out((2, rows, heads_width), BF16, 2), sides_out((2, rows, heads_width), BF16, 2), rows_out((rows, width), BF16, 2)],
            "out_proj",
            flops=4 * rows * width * heads_width,
        )
        norm_stores = [rows_out((rows, width), F32, 4), rows_out((rows, width), BF16, 4), rows_out((rows, 128), F32, 4),
                       Store((2, 128), F32), top_store]
        middle, unit_one, inv_one, sums_one, top = flow(
            partial(norm_body, l, False, 4),
            [whole_in(vecs), pair_in(hidden, other_hidden, 4) if first else rows_in(states, 4), rows_in(part, 4),
             rows_in(core_swap(part), 4, True)],
            norm_stores,
            "norm_one",
        )
        top = over_ranks(top)
        low_mid, fac_mid, active, slope, top = flow(
            partial(up_body, l, 2),
            [whole_in(top), rows_in(middle, 2), whole_in(vecs), layer_in(w_up, l), whole_in(up_near), whole_in(up_far), whole_in(small)],
            [rows_out((rows, width), BF16, 2), rows_out((rows, width), BF16, 2), sides_out((2, rows, units), F32, 2),
             sides_out((2, rows, units), BF16, 2), top_store],
            "up_proj",
            flops=4 * rows * width * units,
        )
        top = over_ranks(top)
        low_act, fac_act, part = flow(
            partial(down_body, 2),
            [whole_in(top), sides_in(active, 2), sides_in(slope, 2), layer_in(w_down, l), whole_in(down_near), whole_in(down_far)],
            [sides_out((2, rows, units), BF16, 2), sides_out((2, rows, units), BF16, 2), rows_out((rows, width), BF16, 2)],
            "down_proj",
            flops=4 * rows * width * units,
        )
        square_terms += [input_sum, sums_one]
        keep = (low_in, fac_in, qkv, ctx, soft, rinv, low_ctx, fac_ctx, unit_one, inv_one, low_mid, fac_mid, low_act, fac_act)
        recv = core_swap(part)
        if not last:
            states, unit_two, inv_two, sums_two, top = flow(
                partial(norm_body, l, True, 4),
                [whole_in(vecs), rows_in(middle, 4), rows_in(part, 4), rows_in(recv, 4, True)],
                norm_stores,
                "norm_two",
            )
            square_terms.append(sums_two)
            input_sum = sums_two[1:2]
            top = over_ranks(top)
            keep += (unit_two, inv_two)
        saved.append(keep)

    other_cotangent = core_swap(cotangent)
    sums = [None] * LAYERS
    band = width // dp_size
    banded = band % 16 == 0

    def add_group(with_ffn, with_attn, ins, name, columns):
        half_width = width // 2
        if banded:
            stores = [Store((width, columns), BF16)] * 2 + [per_side_out((2, half_width, columns), BF16)] * 2
        else:
            stores = [per_side_out((2, width, columns), BF16)] * 2
        return flow(
            partial(grad_body, with_ffn, with_attn, band),
            [whole_in(a) for a in ins],
            stores,
            name,
            flops=4 * rows * width * columns * 2,
            scratch=[pltpu.VMEM((width, columns), F32)],
        )

    def fold_start(group):
        own, oth, keep, send = group
        return own, x_swap(oth), keep, dp_swap(send, 1)

    def fold_second(pending, after=()):
        columns = pending[0].shape[1]
        xkeep, xsend, yown, yoth = run(
            partial(second_kernel, band),
            [full(a) for a in pending],
            [((width // 2, columns), BF16)] * 4,
            "second",
            scratch=[pltpu.VMEM((width, columns), F32)],
            after=after,
        )
        return [xkeep, dp_swap(xsend, 1), yown, x_swap(yoth)]

    def fold_rest(ins):
        remaining = width // 2
        columns = ins[0].shape[-1]
        bit = 2
        while bit < dp_size:
            outs = run(
                partial(fold_kernel, band, bit),
                [full(a) for a in ins],
                [((2, remaining // 2, columns), BF16)] * 2,
                "fold",
                scratch=[pltpu.VMEM((2, remaining, columns), F32)],
            )
            ins = [outs[0], dp_swap(outs[1], bit)]
            remaining //= 2
            bit *= 2
        return ins

    grad_ins = []
    groups = []
    seconds = []
    for l in reversed(range(LAYERS)):
        (low_in, fac_in, qkv, ctx, soft, rinv, low_ctx, fac_ctx, unit_one, inv_one, low_mid, fac_mid, low_act, fac_act) = saved[l][:14]
        (att_near, att_far), (up_near, up_far), (down_near, down_far) = weights[l]
        last = l == LAYERS - 1
        if last:
            ins = [whole_in(vecs), rows_in(middle, 2), rows_in(part, 2), rows_in(recv, 2, True), pair_in(cotangent, other_cotangent, 2)]
            extra = [Store((own_rows, width), BF16), Store((1, 128), F32)]
        else:
            unit_two, inv_two = saved[l][14:]
            ins = [whole_in(vecs), rows_in(part, 2), rows_in(recv, 2, True), rows_in(fac, 2), rows_in(skip, 2), rows_in(unit_two, 2),
                   rows_in(inv_two, 2)]
            extra = []
        dz_two, df, du, part, sums_two, unit_sums, *more = flow(
            partial(ffn_back_body, l, last, 2),
            ins + [sides_in(fac_act, 2), layer_in(w_down, l), whole_in(down_near), whole_in(down_far), layer_in(w_up, l),
                   whole_in(up_near), whole_in(up_far)],
            [rows_out((rows, width), F32, 2), rows_out((rows, width), BF16, 2), sides_out((2, rows, units), BF16, 2),
             rows_out((rows, width), BF16, 2), Store((3, width), F32), Store((2, units), F32)] + extra,
            "ffn_back",
            flops=8 * rows * width * units,
        )
        if last:
            output = more[0]
            square_terms.append(more[1])
        recv = core_swap(part)
        hold = ()
        if banded and groups:
            seconds.append(fold_second(groups.pop(), (du,)))
            hold = (seconds[-1][0],)
        grad_ins = [df, low_act, low_mid, du] + grad_ins
        with_attn = len(grad_ins) > 4
        grads = add_group(True, with_attn, grad_ins, "grads", units + (2 * heads_width if with_attn else 0))
        if banded:
            groups.append(fold_start(grads))
        else:
            groups.append(grads)
        split = l == 0
        dz_one, do, dqkv, sums_one, head_sums, *parts = flow(
            partial(attn_back_body, l, split, 2),
            [whole_in(vecs), rows_in(part, 2), rows_in(recv, 2, True), rows_in(fac_mid, 2), rows_in(dz_two, 2), rows_in(unit_one, 2),
             rows_in(inv_one, 2), layer_in(w_out, l), per_side_in(fac_ctx), per_side_in(rinv), per_side_in(ctx), per_side_in(qkv),
             per_side_in(soft), layer_in(w_qkv, l), whole_in(att_near), whole_in(att_far)],
            [rows_out((rows, width), F32, 2), rows_out((rows, width), BF16, 2), per_side_out((2, rows, 3 * heads_width), BF16),
             Store((3, width), F32), Store((2, 2, heads_width), F32)]
            + ([Store((own_rows, width), BF16)] * 2 if split else [rows_out((rows, width), BF16, 2)]),
            "attn_back",
            flops=6 * rows * rows * 128 * 10,
            scratch=[pltpu.VMEM((rows, width), F32)],
            after=(grads[0],) + hold,
        )
        part = parts[0]
        recv = core_swap(parts[-1])
        fac, skip = fac_in, dz_one
        grad_ins = [low_in, dqkv, do, low_ctx]
        sums[l] = (sums_one, sums_two, head_sums, unit_sums)
    grads = add_group(False, True, grad_ins, "grads", 2 * heads_width)
    groups.append(fold_start(grads) if banded else grads)

    (grad_hidden,) = run(
        dx_kernel,
        [full(part), full(recv), top_rows(fac, own_rows), top_rows(skip, own_rows)],
        [((own_rows, width), F32)],
        "dx",
    )

    if banded:
        folded = []
        for ins in seconds + [fold_second(g) for g in groups]:
            folded += fold_rest(ins)
        grad_qkv, grad_out, grad_up, grad_down = run(
            partial(final_kernel, heads_width),
            [full(a) for a in folded],
            [((LAYERS, 3, band, heads_width), F32), ((LAYERS, band, heads_width), F32), ((LAYERS, band, units), F32),
             ((LAYERS, band, width), F32)],
            "final",
        )
    else:
        totals = []
        for own, oth in groups:
            both = own.astype(F32) + x_swap(oth).astype(F32)
            totals.append(lax.psum_scatter(both, "dp", scatter_dimension=1, tiled=True))
        one, two, three = totals
        grad_up = jnp.stack([two[0, :, :units], one[0]])
        grad_down = jnp.stack([two[1, :, :units], one[1]])
        attn = jnp.stack([three, two[:, :, units:]])
        cut = lambda side, at: attn[:, side, :, at * heads_width : (at + 1) * heads_width]
        grad_qkv = jnp.stack([cut(0, 0), cut(0, 1), cut(1, 0)], 1)
        grad_out = cut(1, 1)

    count_rows = LAYERS * (6 + 2 * tensor_size) + 1
    packed_rows = -(-count_rows // devices) * devices
    (packed,) = run(
        partial(pack_kernel, tensor_size, heads_width),
        [full(a) for l in range(LAYERS) for a in sums[l]] + [full(a) for a in square_terms],
        [((packed_rows, 1, width), F32)],
        "pack",
    )
    chunk = packed_rows // devices
    packed = over_ranks(packed.reshape(devices, chunk, width)).reshape(devices, chunk, width)
    (totals,) = run(total_kernel, [full(packed)], [((devices, chunk, width), F32)], "total")
    totals = over_ranks(totals).reshape(packed_rows, 1, width)
    head_bias, out_bias, gains, shifts, unit_bias, down_bias, rms = run(
        partial(unpack_kernel, tensor_size, heads_width, count_model),
        [full(totals)],
        [(s, F32) for s in ((LAYERS, 2, heads_width), (LAYERS, width), (LAYERS, 2, width), (LAYERS, 2, width), (LAYERS, units),
                            (LAYERS, width), (LAYERS, 3))],
        "unpack",
    )
    return (
        output,
        grad_hidden,
        grad_qkv,
        head_bias,
        jnp.swapaxes(grad_out, 1, 2),
        out_bias,
        gains,
        shifts,
        grad_up,
        unit_bias,
        jnp.swapaxes(grad_down, 1, 2),
        down_bias,
        rms,
    )


def solution(mesh):
    in_specs = (
        P(("dp", "tensor"), None),
        P("dp"),
        P("dp"),
        P(None, None, None, "tensor"),
        P(None, None, "tensor"),
        P(None, "tensor", None),
        P(),
        P(),
        P(),
        P(None, None, "tensor"),
        P(None, "tensor"),
        P(None, "tensor", None),
        P(),
        P(("dp", "tensor"), None),
    )
    out_specs = (
        P(("dp", "tensor"), None),
        P(("dp", "tensor"), None),
        P(None, None, "dp", "tensor"),
        P(None, None, "tensor"),
        P(None, "tensor", "dp"),
        P(),
        P(),
        P(),
        P(None, "dp", "tensor"),
        P(None, "tensor"),
        P(None, "tensor", "dp"),
        P(),
        P(),
    )
    return jax.shard_map(body, mesh=mesh, in_specs=in_specs, out_specs=out_specs, check_vma=False)
```

time: 1350 us -> 488 us (0.36)
  waiting for transfers between devices: 682 us -> 157 us
  blocking collectives: 396 us -> 23.1 us
  Pallas kernels: 0 us -> 208 us
  matrix products: 110 us -> 0 us
  other arithmetic: 66.5 us -> 0 us
  starting transfers between devices: 1.85 us -> 65.3 us
  local copies, waits for them, and re-layouts: 60.3 us -> 22.4 us
  between operations: 23.7 us -> 2.01 us
    reduce_scatter x9 -> x0, waiting for transfers between devices: 362 us -> none  [the longest x4 153 us: forward_rows(): lax.psum_scatter(row_term(jnp.int32(0), row_count * lax.axis_size('tensor...]
    pmax x8 -> x0, blocking collectives: 319 us -> none  [global_top(): return lax.pmax(jnp.max(jnp.abs(values)), ('dp', 'tensor'))]
    pallas_call x0 -> x35, Pallas kernels: none -> 208 us  [the longest x18 150 us: stream(): pl.pallas_call(kernel, in_specs=[pl.BlockSpec(memory_space=pltpu.SMEM)] +...]
    unnamed x23 -> x0, waiting for transfers between devices: 184 us -> none
    all_gather x8 -> x0, waiting for transfers between devices: 136 us -> none  [the longest x4 77.2 us: gather_inputs(): return lax.all_gather(values, 'tensor', axis=0, tiled=True)]
    dot_general x46 -> x0, matrix products: 105 us -> none  [the longest x2 24.6 us: body(): jnp.dot(gathered_mid, w_up[layer_index], preferred_element_type=jnp.float32)]
    ppermute x0 -> x41, waiting for transfers between devices: none -> 95 us  [the longest x13 67.4 us: body(): x_swap = lambda v: lax.ppermute(v, 'tensor', x_pairs)]
    psum x2 -> x0, blocking collectives: 76.8 us -> none  [the longest x1 41.6 us: body(): lax.psum((jnp.stack(out_bias_list), jnp.stack(down_bias_list), jnp.stack(...]
  transfers between devices with their start and end apart: 20 -> 49, of which waited for: 20 -> 26; matrix products, arithmetic and copies ran while one was open for 7% -> 0% of each run, Pallas kernels for 0% -> 31%
where the time goes in v2:
time: 488 us; the launch traced here: 478 us
  Pallas kernels  208 us (43%)
  waiting for transfers between devices  157 us (32%)
  starting transfers between devices  65.3 us (13%)
  blocking collectives  23.1 us (5%)
  local copies, waits for them, and re-layouts  22.4 us (5%)
    pallas_call x18, Pallas kernels, stream(): pl.pallas_call(kernel, in_specs=[pl.BlockSpec(memory_space=pltpu.SMEM)] +...  150 us
    ppermute x13, waiting for transfers between devices, body(): x_swap = lambda v: lax.ppermute(v, 'tensor', x_pairs)  67.4 us
    all_to_all x8, waiting for transfers between devices, body(): over_ranks = lambda top: lax.all_to_all(top, BOTH, 0, 0)  62.2 us
    pallas_call x17, Pallas kernels, run(): pl.pallas_call(trimmed, grid_spec=pltpu.PrefetchScalarGridSpec(num_scalar...  58 us
    all_to_all x8, starting transfers between devices, body(): over_ranks = lambda top: lax.all_to_all(top, BOTH, 0, 0)  29.5 us
    all_to_all x2, blocking collectives, body(): over_ranks = lambda top: lax.all_to_all(top, BOTH, 0, 0)  23.1 us
    ppermute x18, waiting for transfers between devices, body(): lax.ppermute(v, 'dp', [(i, i ^ bit) for i in range(dp_size)])  20.9 us
    unnamed x101, local copies, waits for them, and re-layouts  20.5 us
  transfers between devices with their start and end apart: 49, of which 26 were waited for; matrix products, arithmetic and copies ran while one was open for 0% of the time, Pallas kernels for 31%

profile of v2, /device:TPU:0, one launch (start us, length us, event | category | flops | bytes accessed | tf_op | source)
XLA Modules:
  0.0 478.4 jit_solution(5381112419511859857)
XLA Ops:
  11.7 13.5 %collective-permute-done.1.refs_5_.refs_3_.refs_14_ = bf16[4,192,384]{2,1,0:T(8,128)(2,1)S(1)} collective-permute-done((bf16[4,192,384]{2,1,0:T(8,128)(2,1)}, bf16[4,192,384]{2,1,0:T(8,128)(2,1)S(1)}, u32[]{:S(2)}, u32[]{:S(2)}) %collective-permute-start.1) | collective-permute-done | bytes 589856 | tf_op jit(solution)/shard_map/ppermute | solution.py:825
  40.9 12.6 %attend.2 = (bf16[512,768]{1,0:T(8,128)(2,1)}, bf16[512,768]{1,0:T(8,128)(2,1)}, bf16[2,3,512,192]{3,2,1,0:T(8,128)(2,1)}, f32[2,512,192]{2,1,0:T(8,128)}, bf16[...) custom-call(s32[10]{0:T(128)} %concatenate.3.scal_ref, bf16[256,768]{1,0:T(8,128)(2,1)} %refs_1_.6, ...), custom_call_target="tpu_custom_call" | custom-call | flops 3221225472 | bytes 11313152 | tf_op jit(solution)/shard_map/attend/pallas_call | solution.py:154
  53.5 12.9 %all_to_all.50.refs_0_ = f32[32,1,128]{2,1,0:T(1,128)} all-to-all(f32[32,1,128]{2,1,0:T(1,128)} %get-tuple-element.153.refs_4_), channel_id=1, replica_groups=mesh['dp'=8,'tensor'=4] {'dp','tensor'}, dimensions={0} | all-to-all | bytes 32768 | tf_op jit(solution)/shard_map/all_to_all | solution.py:827
  86.6 12.4 %all-to-all-done.2.refs_0_ = f32[32,1,128]{2,1,0:T(1,128)S(1)} async-done(((f32[32,1,128]{2,1,0:T(1,128)}), f32[32,1,128]{2,1,0:T(1,128)S(1)}, u32[]{:S(2)}, u32[]{:S(2)}) %all-to-all-start.2) | async-done | bytes 16416 | tf_op jit(solution)/shard_map/all_to_all | solution.py:827
  99.6 7.1 %up_proj.2 = (bf16[512,768]{1,0:T(8,128)(2,1)}, bf16[512,768]{1,0:T(8,128)(2,1)}, f32[2,512,768]{2,1,0:T(8,128)}, bf16[2,512,768]{2,1,0:T(8,128)(2,1)}, f32[32,1,128]{2,1,0:T(1,128)}) custom-call(s32[10]{0:T(128)} %concatenate.3.scal_ref, f32[32,1,128]{2,1,0:T(1,128)} %copy-done.42, f32[512,768]{1,0:T(8,128)} %get-tuple-element.156.refs_1_, ...), custom_call_target="tpu_custom_call" | custom-call | flops 1207959552 | bytes 11509760 | tf_op jit(solution)/shard_map/up_proj/pallas_call | solution.py:154
  109.3 7.1 %all-to-all-done.3.refs_0_ = f32[32,1,128]{2,1,0:T(1,128)S(1)} async-done(((f32[32,1,128]{2,1,0:T(1,128)}), f32[32,1,128]{2,1,0:T(1,128)S(1)}, u32[]{:S(2)}, u32[]{:S(2)}) %all-to-all-start.3) | async-done | bytes 16416 | tf_op jit(solution)/shard_map/all_to_all | solution.py:827
  117.1 7.7 %down_proj.2 = (bf16[2,512,768]{2,1,0:T(8,128)(2,1)}, bf16[2,512,768]{2,1,0:T(8,128)(2,1)}, bf16[512,768]{1,0:T(8,128)(2,1)}) custom-call(s32[10]{0:T(128)} %concatenate.3.scal_ref, f32[32,1,128]{2,1,0:T(1,128)} %copy-done.43, f32[2,512,768]{2,1,0:T(8,128)} %get-tuple-element.160.refs_1_, bf16[2,512,768]{2,1,0:T(8,128)(2,1)} %get-tuple-element.161.refs_2_, ...), custom_call_target="tpu_custom_call" | custom-call | flops 1207959552 | bytes 12206080 | tf_op jit(solution)/shard_map/down_proj/pallas_call | solution.py:154
  143.6 12.7 %attend.3 = (bf16[512,768]{1,0:T(8,128)(2,1)}, bf16[512,768]{1,0:T(8,128)(2,1)}, bf16[2,3,512,192]{3,2,1,0:T(8,128)(2,1)}, f32[2,512,192]{2,1,0:T(8,128)}, bf16[...) custom-call(s32[10]{0:T(128)} %concatenate.3.scal_ref, ...), custom_call_target="tpu_custom_call" | custom-call | flops 3221225472 | bytes 12099584 | tf_op jit(solution)/shard_map/attend/pallas_call | solution.py:154
  156.3 10.2 %all_to_all.51.refs_0_ = f32[32,1,128]{2,1,0:T(1,128)} all-to-all(f32[32,1,128]{2,1,0:T(1,128)} %get-tuple-element.167), channel_id=1, replica_groups=mesh['dp'=8,'tensor'=4] {'dp','tensor'}, dimensions={0} | all-to-all | bytes 32768 | tf_op jit(solution)/shard_map/all_to_all | solution.py:827
  186.8 12.4 %all-to-all-done.6.refs_0_ = f32[32,1,128]{2,1,0:T(1,128)S(1)} async-done(((f32[32,1,128]{2,1,0:T(1,128)}), f32[32,1,128]{2,1,0:T(1,128)S(1)}, u32[]{:S(2)}, u32[]{:S(2)}) %all-to-all-start.6) | async-done | bytes 16416 | tf_op jit(solution)/shard_map/all_to_all | solution.py:827
  199.8 7.1 %up_proj.3 = (bf16[512,768]{1,0:T(8,128)(2,1)}, bf16[512,768]{1,0:T(8,128)(2,1)}, f32[2,512,768]{2,1,0:T(8,128)}, bf16[2,512,768]{2,1,0:T(8,128)(2,1)}, f32[32,1,128]{2,1,0:T(1,128)}) custom-call(s32[10]{0:T(128)} %concatenate.3.scal_ref, f32[32,1,128]{2,1,0:T(1,128)} %copy-done.41, f32[512,768]{1,0:T(8,128)} %get-tuple-element.170.refs_1_, ...), custom_call_target="tpu_custom_call" | custom-call | flops 1207959552 | bytes 11509760 | tf_op jit(solution)/shard_map/up_proj/pallas_call | solution.py:154
  211.1 6.7 %all-to-all-done.7.refs_0_ = f32[32,1,128]{2,1,0:T(1,128)S(1)} async-done(((f32[32,1,128]{2,1,0:T(1,128)}), f32[32,1,128]{2,1,0:T(1,128)S(1)}, u32[]{:S(2)}, u32[]{:S(2)}) %all-to-all-start.7) | async-done | bytes 16416 | tf_op jit(solution)/shard_map/all_to_all | solution.py:827
  218.5 7.8 %down_proj.3 = (bf16[2,512,768]{2,1,0:T(8,128)(2,1)}, bf16[2,512,768]{2,1,0:T(8,128)(2,1)}, bf16[512,768]{1,0:T(8,128)(2,1)}) custom-call(s32[10]{0:T(128)} %concatenate.3.scal_ref, f32[32,1,128]{2,1,0:T(1,128)} %copy-done.44, f32[2,512,768]{2,1,0:T(8,128)} %get-tuple-element.174.refs_1_, bf16[2,512,768]{2,1,0:T(8,128)(2,1)} %get-tuple-element.175.refs_2_, ...), custom_call_target="tpu_custom_call" | custom-call | flops 1207959552 | bytes 12206080 | tf_op jit(solution)/shard_map/down_proj/pallas_call | solution.py:154
  230.3 9.8 %ffn_back.2 = (f32[512,768]{1,0:T(8,128)}, bf16[512,768]{1,0:T(8,128)(2,1)}, bf16[2,512,768]{2,1,0:T(8,128)(2,1)}, bf16[512,768]{1,0:T(8,128)(2,1)}, f32[3,768]{...) custom-call(s32[10]{0:T(128)} %concatenate.3.scal_ref, ...), custom_call_target="tpu_custom_call" | custom-call | flops 2415919104 | bytes 17765888 | tf_op jit(solution)/shard_map/ffn_back/pallas_call | solution.py:154
  240.3 7.9 %grads.3 = (bf16[768,768]{1,0:T(8,128)(2,1)}, bf16[768,768]{1,0:T(8,128)(2,1)}, bf16[2,384,768]{2,1,0:T(8,128)(2,1)}, bf16[2,384,768]{2,1,0:T(8,128)(2,1)}) custom-call(s32[10]{0:T(128)} %concatenate.3.scal_ref, bf16[512,768]{1,0:T(8,128)(2,1)} %get-tuple-element.189.refs_0_, bf16[2,512,768]{2,1,0:T(8,128)(2,1)} %get-tuple-element.190.refs_1_, ...), custom_call_target="tpu_custom_call" | custom-call | flops 2415919104 | bytes 9437184 | tf_op jit(solution)/shard_map/grads/pallas_call | solution.py:154
  249.1 14.4 %attn_back.2 = (f32[512,768]{1,0:T(8,128)}, bf16[512,768]{1,0:T(8,128)(2,1)}, bf16[2,512,576]{2,1,0:T(8,128)(2,1)}, f32[3,768]{1,0:T(4,128)}, f32[2,2,192]{2,1,0:T(2,128)}, /*index=5*/bf16[512,768]{1,0:T(8,128)(2,1)}) custom-call(s32[10]{0:T(128)} %concatenate.3.scal_ref, f32[18,768]{1,0:T(8,128)} %get-tuple-element.148.refs_3_.refs_0_.refs_2_, ...), custom_call_target="tpu_custom_call" | custom-call | flops 2013265920 | bytes 19204096 | tf_op jit(solution)/shard_map/attn_back/pallas_call | solution.py:154
  266.9 10.0 %ffn_back.3 = (f32[512,768]{1,0:T(8,128)}, bf16[512,768]{1,0:T(8,128)(2,1)}, bf16[2,512,768]{2,1,0:T(8,128)(2,1)}, bf16[512,768]{1,0:T(8,128)(2,1)}, f32[3,768]{1,0:T(4,128)}, /*index=5*/f32[2,768]{1,0:T(2,128)}) custom-call(s32[10]{0:T(128)} %concatenate.3.scal_ref, f32[18,768]{1,0:T(8,128)} %get-tuple-element.148.refs_3_.refs_0_.refs_2_, ...), custom_call_target="tpu_custom_call" | custom-call | flops 2415919104 | bytes 18420736 | tf_op jit(solution)/shard_map/ffn_back/pallas_call | solution.py:154
  276.9 10.6 %grads.4 = (bf16[768,1152]{1,0:T(8,128)(2,1)}, bf16[768,1152]{1,0:T(8,128)(2,1)}, bf16[2,384,1152]{2,1,0:T(8,128)(2,1)}, bf16[2,384,1152]{2,1,0:T(8,128)(2,1)}) custom-call(s32[10]{0:T(128)} %concatenate.3.scal_ref, bf16[512,768]{1,0:T(8,128)(2,1)} %get-tuple-element.209.refs_0_, bf16[2,512,768]{2,1,0:T(8,128)(2,1)} %get-tuple-element.210.refs_1_, ...), custom_call_target="tpu_custom_call" | custom-call | flops 3623878656 | bytes 14942208 | tf_op jit(solution)/shard_map/grads/pallas_call | solution.py:154
  291.7 37.6 %collective-permute-done.29.refs_1_ = bf16[768,1152]{1,0:T(8,128)(2,1)S(1)} collective-permute-done((bf16[768,1152]{1,0:T(8,128)(2,1)}, bf16[768,1152]{1,0:T(8,128)(2,1)S(1)}, u32[]{:S(2)}, u32[]{:S(2)}) %collective-permute-start.29) | collective-permute-done | bytes 1769504 | tf_op jit(solution)/shard_map/ppermute | solution.py:825
  331.0 6.5 %second.4 = (bf16[384,1152]{1,0:T(8,128)(2,1)}, bf16[384,1152]{1,0:T(8,128)(2,1)}, bf16[384,1152]{1,0:T(8,128)(2,1)}, bf16[384,1152]{1,0:T(8,128)(2,1)}) custom-call(s32[10]{0:T(128)} %concatenate.3.scal_ref, bf16[768,1152]{1,0:T(8,128)(2,1)} %get-tuple-element.217.refs_16_.refs_0_, bf16[768,1152]{1,0:T(8,128)(2,1)} %copy-done.12, ...), custom_call_target="tpu_custom_call" | custom-call | bytes 10616832 | tf_op jit(solution)/shard_map/second/pallas_call | solution.py:847
  339.6 15.0 %collective-permute-done.22.refs_1_ = bf16[768,768]{1,0:T(8,128)(2,1)} collective-permute-done((bf16[768,768]{1,0:T(8,128)(2,1)}, bf16[768,768]{1,0:T(8,128)(2,1)}, u32[]{:S(2)}, u32[]{:S(2)}) %collective-permute-start.22) | collective-permute-done | bytes 1179680 | tf_op jit(solution)/shard_map/ppermute | solution.py:825
  362.3 14.6 %attn_back.3 = (f32[512,768]{1,0:T(8,128)}, bf16[512,768]{1,0:T(8,128)(2,1)}, bf16[2,512,576]{2,1,0:T(8,128)(2,1)}, f32[3,768]{1,0:T(4,128)}, f32[2,2,192]{2,1,0...) custom-call(s32[10]{0:T(128)} %concatenate.3.scal_ref, ...), custom_call_target="tpu_custom_call" | custom-call | flops 2013265920 | bytes 19204096 | tf_op jit(solution)/shard_map/attn_back/pallas_call | solution.py:154
  404.9 6.0 %collective-permute-done.37.refs_1_ = bf16[384,384]{1,0:T(8,128)(2,1)S(1)} collective-permute-done((bf16[384,384]{1,0:T(8,128)(2,1)}, bf16[384,384]{1,0:T(8,128)(2,1)S(1)}, u32[]{:S(2)}, u32[]{:S(2)}) %collective-permute-start.37) | collective-permute-done | bytes 294944 | tf_op jit(solution)/shard_map/ppermute | solution.py:826
  436.6 15.4 %all-to-all-done.8.refs_0_ = f32[32,1,768]{2,1,0:T(1,128)S(1)} async-done(((f32[32,1,768]{2,1,0:T(1,128)}), f32[32,1,768]{2,1,0:T(1,128)S(1)}, u32[]{:S(2)}, u32[]{:S(2)}) %all-to-all-start.8) | async-done | bytes 98336 | tf_op jit(solution)/shard_map/all_to_all | solution.py:827
  (214 shorter events, 198.3 us)
Async XLA Ops:
  33.8 36.6 %collective-permute-start.5 = (bf16[384,768]{1,0:T(8,128)(2,1)}, bf16[384,768]{1,0:T(8,128)(2,1)S(1)}, u32[]{:S(2)}, u32[]{:S(2)}) collective-permute-start(bf16[384,768]{1,0:T(8,128)(2,1)} %get-tuple-element.158), channel_id=1, source_target_pairs={{0,2},{1,3},{2,0},{3,1},{4,6},{5,7},{6,4},{7,5},{8,10},{9,11},{10,... | collective-permute-start | bytes 1769480 | tf_op jit(solution)/shard_map/ppermute | solution.py:825
  34.1 36.9 %collective-permute-start.7 = (bf16[384,768]{1,0:T(8,128)(2,1)}, bf16[384,768]{1,0:T(8,128)(2,1)S(1)}, u32[]{:S(2)}, u32[]{:S(2)}) collective-permute-start(bf16[384,768]{1,0:T(8,128)(2,1)} %get-tuple-element.162), channel_id=1, source_target_pairs={{0,2},{1,3},{2,0},{3,1},{4,6},{5,7},{6,4},{7,5},{8,10},{9,11},{10,... | collective-permute-start | bytes 1769480 | tf_op jit(solution)/shard_map/ppermute | solution.py:825
  71.0 38.4 %collective-permute-start.8 = (bf16[384,768]{1,0:T(8,128)(2,1)S(1)}, bf16[384,768]{1,0:T(8,128)(2,1)S(1)}, u32[]{:S(2)}, u32[]{:S(2)}) collective-permute-start(bf16[384,768]{1,0:T(8,128)(2,1)S(1)} %collective-permute-done.7.refs_4_.refs_9_), channel_id=1, source_target_pairs={{0,4},{4,0},{8,12},{12,8},{16,20},{20,16},{24,28},{28,24},{1,5},{5... | collective-permute-start | bytes 1769480 | tf_op jit(solution)/shard_map/ppermute | solution.py:826
  75.9 48.9 %collective-permute-start.10 = (bf16[4,192,384]{2,1,0:T(8,128)(2,1)}, bf16[4,192,384]{2,1,0:T(8,128)(2,1)S(1)}, u32[]{:S(2)}, u32[]{:S(2)}) collective-permute-start(bf16[4,192,384]{2,1,0:T(8,128)(2,1)} %get-tuple-element.166), channel_id=1, source_target_pairs={{0,2},{1,3},{2,0},{3,1},{4,6},{5,7},{6,4},{7,5},{8,10},{9,11},{10,... | collective-permute-start | bytes 1769480 | tf_op jit(solution)/shard_map/ppermute | solution.py:825
  135.9 34.7 %collective-permute-start.13 = (bf16[384,768]{1,0:T(8,128)(2,1)}, bf16[384,768]{1,0:T(8,128)(2,1)S(1)}, u32[]{:S(2)}, u32[]{:S(2)}) collective-permute-start(bf16[384,768]{1,0:T(8,128)(2,1)} %get-tuple-element.172), channel_id=1, source_target_pairs={{0,2},{1,3},{2,0},{3,1},{4,6},{5,7},{6,4},{7,5},{8,10},{9,11},{10,... | collective-permute-start | bytes 1769480 | tf_op jit(solution)/shard_map/ppermute | solution.py:825
  137.7 33.5 %collective-permute-start.15 = (bf16[384,768]{1,0:T(8,128)(2,1)}, bf16[384,768]{1,0:T(8,128)(2,1)S(1)}, u32[]{:S(2)}, u32[]{:S(2)}) collective-permute-start(bf16[384,768]{1,0:T(8,128)(2,1)} %get-tuple-element.176), channel_id=1, source_target_pairs={{0,2},{1,3},{2,0},{3,1},{4,6},{5,7},{6,4},{7,5},{8,10},{9,11},{10,... | collective-permute-start | bytes 1769480 | tf_op jit(solution)/shard_map/ppermute | solution.py:825
  171.2 39.9 %collective-permute-start.16 = (bf16[384,768]{1,0:T(8,128)(2,1)S(1)}, bf16[384,768]{1,0:T(8,128)(2,1)S(1)}, u32[]{:S(2)}, u32[]{:S(2)}) collective-permute-start(bf16[384,768]{1,0:T(8,128)(2,1)S(1)} %collective-permute-done.15.refs_4_.refs_8_), channel_id=1, source_target_pairs={{0,4},{4,0},{8,12},{12,8},{16,20},{20,16},{24,28},{28,24},{1,5},{5... | collective-permute-start | bytes 1769480 | tf_op jit(solution)/shard_map/ppermute | solution.py:826
  178.8 20.4 %all-to-all-start.6 = ((f32[32,1,128]{2,1,0:T(1,128)}), f32[32,1,128]{2,1,0:T(1,128)S(1)}, u32[]{:S(2)}, u32[]{:S(2)}) async-start(f32[32,1,128]{2,1,0:T(1,128)} %get-tuple-element.171), calls=%async_computation.6 | async-start | bytes 32768 | tf_op jit(solution)/shard_map/all_to_all | solution.py:827
  287.5 41.7 %collective-permute-start.29 = (bf16[768,1152]{1,0:T(8,128)(2,1)}, bf16[768,1152]{1,0:T(8,128)(2,1)S(1)}, u32[]{:S(2)}, u32[]{:S(2)}) collective-permute-start(bf16[768,1152]{1,0:T(8,128)(2,1)} %get-tuple-element.233), channel_id=1, source_target_pairs={{0,2},{1,3},{2,0},{3,1},{4,6},{5,7},{6,4},{7,5},{8,10},{9,11},{10,... | collective-permute-start | bytes 5308424 | tf_op jit(solution)/shard_map/ppermute | solution.py:825
  288.1 41.7 %collective-permute-start.30 = (bf16[2,384,1152]{2,1,0:T(8,128)(2,1)}, bf16[2,384,1152]{2,1,0:T(8,128)(2,1)S(1)}, u32[]{:S(2)}, u32[]{:S(2)}) collective-permute-start(bf16[2,384,1152]{2,1,0:T(8,128)(2,1)} %get-tuple-element.235), channel_id=1, source_target_pairs={{0,4},{4,0},{8,12},{12,8},{16,20},{20,16},{24,28},{28,24},{1,5},{5... | collective-permute-start | bytes 5308424 | tf_op jit(solution)/shard_map/ppermute | solution.py:826
  288.8 65.8 %collective-permute-start.22 = (bf16[768,768]{1,0:T(8,128)(2,1)}, bf16[768,768]{1,0:T(8,128)(2,1)}, u32[]{:S(2)}, u32[]{:S(2)}) collective-permute-start(bf16[768,768]{1,0:T(8,128)(2,1)} %get-tuple-element.218), channel_id=1, source_target_pairs={{0,2},{1,3},{2,0},{3,1},{4,6},{5,7},{6,4},{7,5},{8,10},{9,11},{10,... | collective-permute-start | bytes 3538952 | tf_op jit(solution)/shard_map/ppermute | solution.py:825
  290.2 65.0 %collective-permute-start.23 = (bf16[2,384,768]{2,1,0:T(8,128)(2,1)}, bf16[2,384,768]{2,1,0:T(8,128)(2,1)}, u32[]{:S(2)}, u32[]{:S(2)}) collective-permute-start(bf16[2,384,768]{2,1,0:T(8,128)(2,1)} %get-tuple-element.220), channel_id=1, source_target_pairs={{0,4},{4,0},{8,12},{12,8},{16,20},{20,16},{24,28},{28,24},{1,5},{5... | collective-permute-start | bytes 3538952 | tf_op jit(solution)/shard_map/ppermute | solution.py:826
  291.7 70.6 %collective-permute-start.21 = (bf16[512,768]{1,0:T(8,128)(2,1)}, bf16[512,768]{1,0:T(8,128)(2,1)}, u32[]{:S(2)}, u32[]{:S(2)}) collective-permute-start(bf16[512,768]{1,0:T(8,128)(2,1)} %get-tuple-element.200.refs_1_), channel_id=1, source_target_pairs={{0,1},{1,0},{2,3},{3,2},{4,5},{5,4},{6,7},{7,6},{8,9},{9,8},{10,11... | collective-permute-start | bytes 2359304 | tf_op jit(solution)/shard_map/ppermute | solution.py:824
  337.5 45.9 %collective-permute-start.31 = (bf16[384,1152]{1,0:T(8,128)(2,1)}, bf16[384,1152]{1,0:T(8,128)(2,1)S(1)}, u32[]{:S(2)}, u32[]{:S(2)}) collective-permute-start(bf16[384,1152]{1,0:T(8,128)(2,1)} %get-tuple-element.237), channel_id=1, source_target_pairs={{0,4},{4,0},{8,12},{12,8},{16,20},{20,16},{24,28},{28,24},{1,5},{5... | collective-permute-start | bytes 2654216 | tf_op jit(solution)/shard_map/ppermute | solution.py:826
  338.2 46.6 %collective-permute-start.32 = (bf16[384,1152]{1,0:T(8,128)(2,1)}, bf16[384,1152]{1,0:T(8,128)(2,1)S(1)}, u32[]{:S(2)}, u32[]{:S(2)}) collective-permute-start(bf16[384,1152]{1,0:T(8,128)(2,1)} %get-tuple-element.239), channel_id=1, source_target_pairs={{0,2},{1,3},{2,0},{3,1},{4,6},{5,7},{6,4},{7,5},{8,10},{9,11},{10,... | collective-permute-start | bytes 2654216 | tf_op jit(solution)/shard_map/ppermute | solution.py:825
  360.2 30.7 %collective-permute-start.25 = (bf16[384,768]{1,0:T(8,128)(2,1)}, bf16[384,768]{1,0:T(8,128)(2,1)S(1)}, u32[]{:S(2)}, u32[]{:S(2)}) collective-permute-start(bf16[384,768]{1,0:T(8,128)(2,1)} %get-tuple-element.226), channel_id=1, source_target_pairs={{0,4},{4,0},{8,12},{12,8},{16,20},{20,16},{24,28},{28,24},{1,5},{5... | collective-permute-start | bytes 1769480 | tf_op jit(solution)/shard_map/ppermute | solution.py:826
  360.9 30.1 %collective-permute-start.26 = (bf16[384,768]{1,0:T(8,128)(2,1)}, bf16[384,768]{1,0:T(8,128)(2,1)S(1)}, u32[]{:S(2)}, u32[]{:S(2)}) collective-permute-start(bf16[384,768]{1,0:T(8,128)(2,1)} %get-tuple-element.228), channel_id=1, source_target_pairs={{0,2},{1,3},{2,0},{3,1},{4,6},{5,7},{6,4},{7,5},{8,10},{9,11},{10,... | collective-permute-start | bytes 1769480 | tf_op jit(solution)/shard_map/ppermute | solution.py:825
  390.3 25.0 %collective-permute-start.33 = (bf16[2,192,1152]{2,1,0:T(8,128)(2,1)}, bf16[2,192,1152]{2,1,0:T(8,128)(2,1)S(1)}, u32[]{:S(2)}, u32[]{:S(2)}) collective-permute-start(bf16[2,192,1152]{2,1,0:T(8,128)(2,1)} %get-tuple-element.241), channel_id=1, source_target_pairs={{0,8},{4,12},{8,0},{12,4},{16,24},{20,28},{24,16},{28,20},{1,9},{5... | collective-permute-start | bytes 2654216 | tf_op jit(solution)/shard_map/ppermute | solution.py:826
  395.7 37.1 %collective-permute-start.27 = (bf16[2,192,768]{2,1,0:T(8,128)(2,1)}, bf16[2,192,768]{2,1,0:T(8,128)(2,1)S(1)}, u32[]{:S(2)}, u32[]{:S(2)}) collective-permute-start(bf16[2,192,768]{2,1,0:T(8,128)(2,1)} %get-tuple-element.230), channel_id=1, source_target_pairs={{0,8},{4,12},{8,0},{12,4},{16,24},{20,28},{24,16},{28,20},{1,9},{5... | collective-permute-start | bytes 1769480 | tf_op jit(solution)/shard_map/ppermute | solution.py:826
  414.7 42.7 %collective-permute-start.39 = (bf16[2,192,384]{2,1,0:T(8,128)(2,1)}, bf16[2,192,384]{2,1,0:T(8,128)(2,1)S(1)}, u32[]{:S(2)}, u32[]{:S(2)}) collective-permute-start(bf16[2,192,384]{2,1,0:T(8,128)(2,1)} %get-tuple-element.257), channel_id=1, source_target_pairs={{0,8},{4,12},{8,0},{12,4},{16,24},{20,28},{24,16},{28,20},{1,9},{5... | collective-permute-start | bytes 884744 | tf_op jit(solution)/shard_map/ppermute | solution.py:826
  419.6 52.5 %collective-permute-start.34 = (bf16[2,96,1152]{2,1,0:T(8,128)(2,1)}, bf16[2,96,1152]{2,1,0:T(8,128)(2,1)S(1)}, u32[]{:S(2)}, u32[]{:S(2)}) collective-permute-start(bf16[2,96,1152]{2,1,0:T(8,128)(2,1)} %get-tuple-element.243), channel_id=1, source_target_pairs={{0,16},{4,20},{8,24},{12,28},{16,0},{20,4},{24,8},{28,12},{1,17},{... | collective-permute-start | bytes 1327112 | tf_op jit(solution)/shard_map/ppermute | solution.py:826
  420.2 48.0 %collective-permute-start.24 = (bf16[256,768]{1,0:T(8,128)(2,1)S(1)}, bf16[256,768]{1,0:T(8,128)(2,1)S(1)}, u32[]{:S(2)}, u32[]{:S(2)}) collective-permute-start(bf16[256,768]{1,0:T(8,128)(2,1)S(1)} %copy-done.48), channel_id=1, source_target_pairs={{0,1},{1,0},{2,3},{3,2},{4,5},{5,4},{6,7},{7,6},{8,9},{9,8},{10,11... | collective-permute-start | bytes 1179656 | tf_op jit(solution)/shard_map/ppermute | solution.py:824
  422.9 29.1 %all-to-all-start.8 = ((f32[32,1,768]{2,1,0:T(1,128)}), f32[32,1,768]{2,1,0:T(1,128)S(1)}, u32[]{:S(2)}, u32[]{:S(2)}) async-start(f32[32,1,768]{2,1,0:T(1,128)} %pack.1), calls=%async_computation.8 | async-start | bytes 196608 | tf_op jit(solution)/shard_map/all_to_all | solution.py:827
  436.6 35.5 %collective-permute-start.28 = (bf16[2,96,768]{2,1,0:T(8,128)(2,1)}, bf16[2,96,768]{2,1,0:T(8,128)(2,1)S(1)}, u32[]{:S(2)}, u32[]{:S(2)}) collective-permute-start(bf16[2,96,768]{2,1,0:T(8,128)(2,1)} %get-tuple-element.232), channel_id=1, source_target_pairs={{0,16},{4,20},{8,24},{12,28},{16,0},{20,4},{24,8},{28,12},{1,17},{... | collective-permute-start | bytes 884744 | tf_op jit(solution)/shard_map/ppermute | solution.py:826
  (75 other events, 466.1 us)
